TPU v7x, 128 devices: a whole 4x4x4 slice. The times are simulated.
128 devices in a mesh: dp: 16 (over z_lo, x, core), seq: 8 (over y, z_hi).
Axes of the slice: x: 4, y: 4, z: 4 (z_hi: 2, z_lo: 2; z = z_hi * 2 + z_lo), core: 2. Of those that a mesh axis runs over, the one named last changes fastest.
Arguments:
- hidden_in: bfloat16 [16, 1024, 2048], P('dp', 'seq'), may hold values from -6 to 6
- norm1_gain: bfloat16 [2048], P(('dp', 'seq')), may hold values from 0.099609375 to 1.8984375
- query_weight: bfloat16 [2048, 256], P(('dp', 'seq')), may hold values from -0.125 to 0.125
- key_weight: bfloat16 [2048, 256], P(('dp', 'seq')), may hold values from -0.125 to 0.125
- value_weight: bfloat16 [2048, 2048], P(('dp', 'seq')), may hold values from -0.125 to 0.125
- out_weight: bfloat16 [2048, 2048], P(('dp', 'seq')), may hold values from -1 to 1
- norm2_gain: bfloat16 [2048], P(('dp', 'seq')), may hold values from 0.099609375 to 1.8984375
- gate_weight: bfloat16 [2048, 5504], P(('dp', 'seq')), may hold values from -0.125 to 0.125
- up_weight: bfloat16 [2048, 5504], P(('dp', 'seq')), may hold values from -0.125 to 0.125
- down_weight: bfloat16 [2048, 5504], P(('dp', 'seq')), may hold values from -0.078125 to 0.078125
- cotangent: bfloat16 [16, 1024, 2048], P('dp', 'seq'), may hold values from -6 to 6
- source_id: int32 [16], P('dp'), may hold values from 0 to 7
- source_counts: int32 [8], replicated, may hold values from 1 to 64
Outputs:
- layer_out: bfloat16 [16, 1024, 2048], P('dp', 'seq')
- grad_in: float32 [16, 1024, 2048], P('dp', 'seq')
- grad_norm1: float32 [2048], P(('dp', 'seq'))
- grad_query: float32 [2048, 256], P(('dp', 'seq'))
- grad_key: float32 [2048, 256], P(('dp', 'seq'))
- grad_value: float32 [2048, 2048], P(('dp', 'seq'))
- grad_out: float32 [2048, 2048], P(('dp', 'seq'))
- grad_norm2: float32 [2048], P(('dp', 'seq'))
- grad_gate: float32 [2048, 5504], P(('dp', 'seq'))
- grad_up: float32 [2048, 5504], P(('dp', 'seq'))
- grad_down: float32 [2048, 5504], P(('dp', 'seq'))
All inputs are finite; a program needn't handle non-finite values.
Results may differ from a plain program's by a relative error of at most 0.025.
Values may be sent and summed in bfloat16 or wider, within the bound.
A program may use at most 192 MiB of HBM per device.

v0:
```python
import math

import jax
import jax.numpy as jnp
from jax import lax
from jax.sharding import PartitionSpec as P

FEAT = 16
HEAD_V = 128


norm_eps = 1e-05


def side_by_side(arrays, axis, dim, along):
    widths = [a.shape[along] for a in arrays]
    both = jnp.concatenate(arrays, axis=along)
    filled = lax.all_gather(both, axis, axis=dim, tiled=True)
    return tuple(jnp.split(filled, [sum(widths[:k]) for k in range(1, len(widths))], axis=along))


def sent_together(arrays, axis, dim, along):
    ends, at = ([], 0)
    for a in arrays[:-1]:
        at += a.shape[along]
        ends.append(at)
    both = jnp.concatenate(arrays, axis=along)
    return tuple(
        jnp.split(lax.psum_scatter(both, axis, scatter_dimension=dim, tiled=True), ends, axis=along)
    )


def taylor(inputs):
    inner = inputs.shape[-1]
    lead = inputs.shape[:-1]
    first = inputs / inner**0.25
    second = (inputs[..., :, None] * inputs[..., None, :]).reshape(
        lead + (inner * inner,)
    ) / math.sqrt(2.0 * inner)
    return jnp.concatenate([jnp.ones(lead + (1,), jnp.float32), first, second], axis=-1)


def contract_rows(left, right):
    return lax.dot_general(
        left, right, (((0,), (0,)), ((), ())), preferred_element_type=jnp.float32
    )


def contract_cols(left, right):
    return lax.dot_general(
        left, right, (((1,), (1,)), ((), ())), preferred_element_type=jnp.float32
    )


def norm_back(grad_normed, inputs, inverse, gain):
    unit = inputs * inverse
    scaled = grad_normed * gain
    grad_gain = jnp.sum(grad_normed * unit, axis=0)
    grad_inputs = inverse * (scaled - unit * jnp.mean(scaled * unit, axis=-1, keepdims=True))
    return (grad_inputs, grad_gain)


def mlp_front(normed_in, w_gate, w_up):
    gate = jnp.dot(normed_in, w_gate, preferred_element_type=jnp.float32)
    upward = jnp.dot(normed_in, w_up, preferred_element_type=jnp.float32)
    hidden = (jax.nn.silu(gate) * upward).astype(jnp.bfloat16)
    return (gate, upward, hidden)


def causal_mask(toks):
    return jnp.arange(toks)[:, None] >= jnp.arange(toks)[None, :]


def attend(feat_q, feat_k, values):
    causal = causal_mask(feat_q.shape[1])
    scores = jnp.einsum("rthf,rshf->rhts", feat_q, feat_k, preferred_element_type=jnp.float32)
    scores = jnp.where(causal, scores, 0.0)
    numer = jnp.einsum("rhts,rshv->rthv", scores, values.astype(jnp.float32))
    denom = jnp.swapaxes(jnp.sum(scores, axis=-1), 1, 2)
    return (scores, denom, numer / denom[..., None])


def attend_back(grad_mixed, scores, denom, mixed, feat_q, feat_k, values):
    causal = causal_mask(feat_q.shape[1])
    grad_numer = grad_mixed / denom[..., None]
    grad_denom = -jnp.sum(grad_mixed * mixed, axis=-1) / denom
    query_wide = feat_q.astype(jnp.float32)
    key_wide = feat_k.astype(jnp.float32)
    values_wide = values.astype(jnp.float32)
    grad_scores = jnp.einsum("rthv,rshv->rhts", grad_numer, values_wide)
    grad_scores = jnp.where(causal, grad_scores + jnp.swapaxes(grad_denom, 1, 2)[..., None], 0.0)
    grad_feat_q = jnp.einsum("rhts,rshf->rthf", grad_scores, key_wide)
    grad_feat_k = jnp.einsum("rhts,rthf->rshf", grad_scores, query_wide)
    grad_values = jnp.einsum("rhts,rthv->rshv", scores, grad_numer)
    return (grad_numer, grad_denom, grad_feat_q, grad_feat_k, grad_values)


def feature_back(query, keys, grad_feat_q, grad_feat_k, count):
    unused_q, pull_query = jax.vjp(taylor, query)
    grad_q = pull_query(grad_feat_q)[0].astype(jnp.bfloat16).reshape(count, -1)
    unused_k, pull_keys = jax.vjp(taylor, keys)
    grad_k = pull_keys(grad_feat_k)[0].astype(jnp.bfloat16).reshape(count, -1)
    return (grad_q, grad_k)


def scaled_top(cotangent, source_id, source_counts, count, width):
    picked = jnp.sum(
        jnp.where(
            source_id[:, None] == jnp.arange(source_counts.shape[0], dtype=jnp.int32)[None, :],
            source_counts[None, :],
            0,
        ),
        axis=1,
    )
    row_scale = 4.0 / jnp.sqrt(picked.astype(jnp.float32))
    return (cotangent.astype(jnp.float32) * row_scale[:, None, None]).reshape(count, width)


def whole_row(piece):
    return lax.all_gather(piece, "seq", axis=0, tiled=True)


def own_rows(pairs):
    total = None
    for left, right in pairs:
        part = contract_cols(left, right)
        total = part if total is None else total + part
    return lax.psum_scatter(total, "seq", scatter_dimension=0, tiled=True)


def column_plan(
    hidden_in,
    norm1_gain,
    query_weight,
    key_weight,
    value_weight,
    out_weight,
    norm2_gain,
    gate_weight,
    up_weight,
    down_weight,
    cotangent,
    source_id,
    source_counts,
):
    rows, toks, width = hidden_in.shape
    count = rows * toks
    seq_count = lax.axis_size("seq")
    gain_pair = jnp.stack((norm1_gain, norm2_gain), axis=1)
    gain_wide = jnp.tile(gain_pair, (1, seq_count))
    spread = (
        lax.all_to_all(query_weight, "seq", split_axis=1, concat_axis=0, tiled=True),
        lax.all_to_all(key_weight, "seq", split_axis=1, concat_axis=0, tiled=True),
        lax.all_to_all(value_weight, "seq", split_axis=1, concat_axis=0, tiled=True),
        lax.all_to_all(out_weight, "seq", split_axis=1, concat_axis=0, tiled=True),
        lax.all_to_all(gate_weight, "seq", split_axis=1, concat_axis=0, tiled=True),
        lax.all_to_all(up_weight, "seq", split_axis=1, concat_axis=0, tiled=True),
        lax.all_to_all(down_weight, "seq", split_axis=1, concat_axis=0, tiled=True),
        lax.all_to_all(gain_wide, "seq", split_axis=1, concat_axis=0, tiled=True),
    )
    w_query, w_key, w_value, w_out, w_gate, w_up, w_down, gain_cols = side_by_side(
        (spread[0], spread[1], spread[2], spread[3], spread[4], spread[5], spread[6], spread[7]),
        "dp",
        0,
        1,
    )
    norm1 = gain_cols[:, 0].astype(jnp.float32)
    norm2 = gain_cols[:, 1].astype(jnp.float32)
    heads_here = w_query.shape[1] // FEAT
    inputs = hidden_in.astype(jnp.float32).reshape(count, width)
    inverse1 = lax.rsqrt(jnp.mean(inputs * inputs, axis=-1, keepdims=True) + norm_eps)
    normed = whole_row((inputs * inverse1 * norm1).astype(jnp.bfloat16))
    length = normed.shape[0]
    query = jnp.dot(normed, w_query, preferred_element_type=jnp.float32).reshape(
        1, length, heads_here, FEAT
    )
    keys = jnp.dot(normed, w_key, preferred_element_type=jnp.float32).reshape(
        1, length, heads_here, FEAT
    )
    values = jnp.dot(normed, w_value, preferred_element_type=jnp.float32).astype(jnp.bfloat16)
    values = values.reshape(1, length, heads_here, HEAD_V)
    feat_q = taylor(query).astype(jnp.bfloat16)
    feat_k = taylor(keys).astype(jnp.bfloat16)
    scores, denom, mixed = attend(feat_q, feat_k, values)
    attended = mixed.astype(jnp.bfloat16).reshape(length, heads_here * HEAD_V)
    middle = inputs + own_rows(((attended, w_out),))
    inverse2 = lax.rsqrt(jnp.mean(middle * middle, axis=-1, keepdims=True) + norm_eps)
    normed2 = whole_row((middle * inverse2 * norm2).astype(jnp.bfloat16))
    gate, upward, hidden = mlp_front(normed2, w_gate, w_up)
    layer_out = (
        (middle + own_rows(((hidden, w_down),))).astype(jnp.bfloat16).reshape(rows, toks, width)
    )
    grad_top = scaled_top(cotangent, source_id, source_counts, count, width)
    grad_low = whole_row(grad_top.astype(jnp.bfloat16))
    gate, upward, hidden = mlp_front(normed2, w_gate, w_up)
    grad_down = contract_rows(grad_low, hidden)
    grad_hidden = jnp.dot(grad_low, w_down, preferred_element_type=jnp.float32)
    sigma = jax.nn.sigmoid(gate)
    gate_act = (grad_hidden * upward * sigma * (1.0 + gate * (1.0 - sigma))).astype(jnp.bfloat16)
    up_act = (grad_hidden * gate * sigma).astype(jnp.bfloat16)
    grad_gate = contract_rows(normed2, gate_act)
    grad_up = contract_rows(normed2, up_act)
    grad_normed2 = own_rows(((gate_act, w_gate), (up_act, w_up)))
    grad_mid_norm, grad_norm2 = norm_back(grad_normed2, middle, inverse2, norm2)
    grad_middle = grad_top + grad_mid_norm
    middle_low = whole_row(grad_middle.astype(jnp.bfloat16))
    grad_out = contract_rows(middle_low, attended)
    grad_mixed = lax.optimization_barrier(
        jnp.dot(middle_low, w_out, preferred_element_type=jnp.float32).astype(jnp.bfloat16)
    ).astype(jnp.float32)
    grad_mixed = grad_mixed.reshape(1, length, heads_here, HEAD_V)
    grad_numer, grad_denom, grad_feat_q, grad_feat_k, grad_values = attend_back(
        grad_mixed, scores, denom, mixed, feat_q, feat_k, values
    )
    grad_values = grad_values.astype(jnp.bfloat16).reshape(length, heads_here * HEAD_V)
    grad_q, grad_k = feature_back(query, keys, grad_feat_q, grad_feat_k, length)
    grad_query = contract_rows(normed, grad_q)
    grad_key = contract_rows(normed, grad_k)
    grad_value = contract_rows(normed, grad_values)
    grad_normed = own_rows(((grad_q, w_query), (grad_k, w_key), (grad_values, w_value)))
    grad_in_norm, grad_norm1 = norm_back(grad_normed, inputs, inverse1, norm1)
    grad_in = (grad_middle + grad_in_norm).reshape(rows, toks, width)
    grad_pair = jnp.stack((grad_norm1, grad_norm2), axis=1)
    summed = tuple(
        (
            part.astype(jnp.float32)
            for part in sent_together(
                (
                    grad_query.astype(jnp.bfloat16),
                    grad_key.astype(jnp.bfloat16),
                    grad_value.astype(jnp.bfloat16),
                    grad_out.astype(jnp.bfloat16),
                    grad_gate.astype(jnp.bfloat16),
                    grad_up.astype(jnp.bfloat16),
                    grad_down.astype(jnp.bfloat16),
                    grad_pair.astype(jnp.bfloat16),
                ),
                "dp",
                0,
                1,
            )
        )
    )
    joined = (
        lax.all_to_all(
            summed[0].astype(jnp.bfloat16), "seq", split_axis=0, concat_axis=1, tiled=True
        ).astype(jnp.float32),
        lax.all_to_all(
            summed[1].astype(jnp.bfloat16), "seq", split_axis=0, concat_axis=1, tiled=True
        ).astype(jnp.float32),
        lax.all_to_all(
            summed[2].astype(jnp.bfloat16), "seq", split_axis=0, concat_axis=1, tiled=True
        ).astype(jnp.float32),
        lax.all_to_all(
            summed[3].astype(jnp.bfloat16), "seq", split_axis=0, concat_axis=1, tiled=True
        ).astype(jnp.float32),
        lax.all_to_all(
            summed[4].astype(jnp.bfloat16), "seq", split_axis=0, concat_axis=1, tiled=True
        ).astype(jnp.float32),
        lax.all_to_all(
            summed[5].astype(jnp.bfloat16), "seq", split_axis=0, concat_axis=1, tiled=True
        ).astype(jnp.float32),
        lax.all_to_all(
            summed[6].astype(jnp.bfloat16), "seq", split_axis=0, concat_axis=1, tiled=True
        ).astype(jnp.float32),
        lax.all_to_all(
            summed[7].astype(jnp.bfloat16), "seq", split_axis=0, concat_axis=1, tiled=True
        ).astype(jnp.float32),
    )
    pair_cols = joined[7]
    pair_sum = jnp.sum(pair_cols.reshape(pair_cols.shape[0], seq_count, 2), axis=1)
    gain_one = pair_sum[:, 0]
    gain_two = pair_sum[:, 1]
    return (
        layer_out,
        grad_in,
        gain_one,
        joined[0],
        joined[1],
        joined[2],
        joined[3],
        gain_two,
        joined[4],
        joined[5],
        joined[6],
    )


def body(
    hidden_in,
    norm1_gain,
    query_weight,
    key_weight,
    value_weight,
    out_weight,
    norm2_gain,
    gate_weight,
    up_weight,
    down_weight,
    cotangent,
    source_id,
    source_counts,
):
    return column_plan(
        hidden_in,
        norm1_gain,
        query_weight,
        key_weight,
        value_weight,
        out_weight,
        norm2_gain,
        gate_weight,
        up_weight,
        down_weight,
        cotangent,
        source_id,
        source_counts,
    )


def solution(mesh):
    return jax.shard_map(
        body,
        mesh=mesh,
        in_specs=(
            P("dp", "seq", None),
            P(("dp", "seq")),
            P(("dp", "seq"), None),
            P(("dp", "seq"), None),
            P(("dp", "seq"), None),
            P(("dp", "seq"), None),
            P(("dp", "seq")),
            P(("dp", "seq"), None),
            P(("dp", "seq"), None),
            P(("dp", "seq"), None),
            P("dp", "seq", None),
            P("dp"),
            P(),
        ),
        out_specs=(
            P("dp", "seq", None),
            P("dp", "seq", None),
            P(("dp", "seq")),
            P(("dp", "seq"), None),
            P(("dp", "seq"), None),
            P(("dp", "seq"), None),
            P(("dp", "seq"), None),
            P(("dp", "seq")),
            P(("dp", "seq"), None),
            P(("dp", "seq"), None),
            P(("dp", "seq"), None),
        ),
        check_vma=False,
    )
```

profile of v0, /device:TPU:1, one launch (start us, length us, event | category | flops | bytes accessed | tf_op | source)
XLA Modules:
  0.0 1168.3 jit_solution(11930578180683126701)
XLA Ops:
  8.5 8.3 all-to-all-start.7
  77.5 5.9 all-to-all-done.5
  87.2 6.6 all-to-all-done.6
  95.3 71.9 %all-gather.6.cloned.1.call-done = bf16[2048,2642]{1,0:T(8,128)(2,1)} async-done(((bf16[128,2642]{1,0:T(8,128)(2,1)}), bf16[2048,2642]{1,0:T(8,128)(2,1)}) %all-gather.6.cloned.1.call-update) | async-done | bytes 10821648 | tf_op jit(solution)/shard_map/all_gather | solution.py:18
  171.8 70.2 %all-gather.8.cloned.1.call-done = bf16[1024,2048]{1,0:T(8,128)(2,1)} async-done(((bf16[128,2048]{1,0:T(8,128)(2,1)}), bf16[1024,2048]{1,0:T(8,128)(2,1)}) %all-gather.8.cloned.1.call-update) | async-done | bytes 4194320 | tf_op jit(solution)/shard_map/all_gather | solution.py:120
  259.5 6.5 fusion.51
  266.2 112.4 %reduce-scatter.8.cloned.1.call-done = f32[128,2048]{1,0:T(8,128)} async-done(((f32[1024,2048]{1,0:T(8,128)}), f32[128,2048]{1,0:T(8,128)}) %reduce-scatter.8.cloned.1.call-update) | async-done | bytes 1048592 | tf_op jit(solution)/shard_map/reduce_scatter | solution.py:128
  384.2 66.3 %all-gather.10.cloned.1.call-done = bf16[1024,2048]{1,0:T(8,128)(2,1)} async-done(((bf16[128,2048]{1,0:T(8,128)(2,1)}), bf16[1024,2048]{1,0:T(8,128)(2,1)}) %all-gather.10.cloned.1.call-update) | async-done | bytes 4194320 | tf_op jit(solution)/shard_map/all_gather | solution.py:120
  450.6 8.9 fusion.21
  459.4 7.8 fusion.25
  467.2 54.9 %all-gather.12.cloned.1.call-done = bf16[1024,2048]{1,0:T(8,128)(2,1)} async-done(((bf16[128,2048]{1,0:T(8,128)(2,1)}), bf16[1024,2048]{1,0:T(8,128)(2,1)}) %all-gather.12.cloned.1.call-update) | async-done | bytes 4194320 | tf_op jit(solution)/shard_map/all_gather | solution.py:120
  522.1 11.4 multiply_convert_fusion
  533.5 7.7 fusion.23
  541.2 9.8 convolution_add_fusion
  551.0 112.2 %reduce-scatter.12.cloned.1.call-done = f32[128,2048]{1,0:T(8,128)} async-done(((f32[1024,2048]{1,0:T(8,128)}), f32[128,2048]{1,0:T(8,128)}) %reduce-scatter.12.cloned.1.call-update) | async-done | bytes 1048592 | tf_op jit(solution)/shard_map/reduce_scatter | solution.py:128
  667.4 69.4 %all-gather.14.cloned.1.call-done = bf16[1024,2048]{1,0:T(8,128)(2,1)} async-done(((bf16[128,2048]{1,0:T(8,128)(2,1)}), bf16[1024,2048]{1,0:T(8,128)(2,1)}) %all-gather.14.cloned.1.call-update) | async-done | bytes 4194320 | tf_op jit(solution)/shard_map/all_gather | solution.py:120
  760.2 6.4 add_add_fusion
  766.6 10.4 fusion.18
  777.1 7.4 convolution_convert_fusion
  799.5 79.1 %reduce-scatter.14.cloned.1.call-done = f32[128,2048]{1,0:T(8,128)} async-done(((f32[1024,2048]{1,0:T(8,128)}), f32[128,2048]{1,0:T(8,128)}) %reduce-scatter.14.cloned.1.call-update) | async-done | bytes 1048592 | tf_op jit(solution)/shard_map/reduce_scatter | solution.py:128
  880.2 47.6 %concatenate.29 = bf16[2048,2642]{0,1:T(8,128)(2,1)} concatenate(bf16[2048,32]{0,1:T(8,128)(2,1)S(1)} %convolution_convert_fusion.6, bf16[2048,32]{0,1:T(8,128)(2,1)S(1)} %convolution_convert_fusion.5, bf16[2048,256]{0,1:T(8,128)(2,1)} %convolution_convert_fusion.4, bf16[2048,256]{0,1:T(8,128)(2,1)S(1)} %convolution_convert_fusion.3, ...), dimensions={1} | concatenate | bytes 21643264 | tf_op jit(solution)/shard_map/concatenate | solution.py:27
  927.8 14.3 %copy.134 = bf16[2048,2642]{1,0:T(8,128)(2,1)} copy(bf16[2048,2642]{0,1:T(8,128)(2,1)} %concatenate.29) | data formatting | bytes 21643264
  942.2 52.6 %reduce-scatter.10.cloned.1.call-done = f32[128,2048]{1,0:T(8,128)} async-done(((f32[1024,2048]{1,0:T(8,128)}), f32[128,2048]{1,0:T(8,128)}) %reduce-scatter.10.cloned.1.call-update) | async-done | bytes 1048592 | tf_op jit(solution)/shard_map/reduce_scatter | solution.py:128
  997.9 73.8 %reduce-scatter.16.cloned.1.call-done = bf16[128,2642]{1,0:T(8,128)(2,1)} async-done(((bf16[2048,2642]{1,0:T(8,128)(2,1)}), bf16[128,2642]{1,0:T(8,128)(2,1)}) %reduce-scatter.16.cloned.1.call-update) | async-done | bytes 676368 | tf_op jit(solution)/shard_map/reduce_scatter | solution.py:29
  1073.3 6.0 all-to-all-start.8
  1085.8 6.4 all-to-all-start.9
  1092.7 6.0 all-to-all-done.9
  1102.1 6.3 all-to-all-done.10
  1122.4 5.9 all-to-all-done.11
  1132.4 6.3 all-to-all-done.13
  1143.3 6.2 all-to-all-done.15
  1154.1 6.0 all-to-all-done.14
  (199 shorter events, 181.1 us)
Async XLA Ops:
  7.2 69.2 %copy-start.18 = (bf16[16,5504]{1,0:T(8,128)(2,1)S(1)}, bf16[16,5504]{1,0:T(8,128)(2,1)}, u32[]{:S(2)}) copy-start(bf16[16,5504]{1,0:T(8,128)(2,1)} %param.22) | copy-start | bytes 528388
  8.5 14.8 %all-to-all-start.7 = ((bf16[16,8,2]{0,2,1:T(2,128)(2,1)}), bf16[16,8,2]{0,2,1:T(2,128)(2,1)S(1)}, u32[]{:S(2)}, u32[]{:S(2)}) async-start(bf16[16,8,2]{0,2,1:T(2,128)(2,1)} %tile.2), calls=%async_computation.7 | async-start | bytes 8192 | tf_op jit(solution)/shard_map/all_to_all | solution.py:159
  23.3 9.8 all-to-all-start
  33.1 9.8 all-to-all-start.1
  36.4 58.7 %copy-start.2 = (bf16[1,128,2048]{2,1,0:T(8,128)(2,1)S(1)}, bf16[1,128,2048]{2,1,0:T(8,128)(2,1)}, u32[]{:S(2)}) copy-start(bf16[1,128,2048]{2,1,0:T(8,128)(2,1)} %param.13) | copy-start | bytes 1572868
  42.9 9.9 all-to-all-start.2
  52.8 9.9 all-to-all-start.3
  62.7 10.4 all-to-all-start.4
  73.0 10.4 all-to-all-start.5
  83.4 10.4 all-to-all-start.6
  86.8 80.5 %all-gather.6.cloned.1.call-start = ((), (), s32[]{:S(2)}) async-start(), calls=%async_computation.21 | async-start | bytes 11698176 | tf_op jit(solution)/shard_map/all_gather | solution.py:18
  95.1 147.0 %all-gather.8.cloned.1.call-start = ((), (), s32[]{:S(2)}) async-start(), calls=%async_computation.22 | async-start | bytes 4718592 | tf_op jit(solution)/shard_map/all_gather | solution.py:120
  170.3 208.2 %reduce-scatter.8.cloned.1.call-start = ((), (), s32[]{:S(2)}) async-start(), calls=%async_computation.23 | async-start | bytes 9437184 | tf_op jit(solution)/shard_map/reduce_scatter | solution.py:128
  266.1 115.6 %copy-start.24 = (s32[8]{0:T(128)S(1)}, s32[8]{0:T(128)}, u32[]{:S(2)}) copy-start(s32[8]{0:T(128)} %param.25) | copy-start | bytes 100
  266.1 116.9 %copy-start.4 = (bf16[1,128,2048]{2,1,0:T(8,128)(2,1)S(1)}, bf16[1,128,2048]{2,1,0:T(8,128)(2,1)}, u32[]{:S(2)}) copy-start(bf16[1,128,2048]{2,1,0:T(8,128)(2,1)} %param.23) | copy-start | bytes 1572868
  266.1 184.4 %all-gather.10.cloned.1.call-start = ((), (), s32[]{:S(2)}) async-start(), calls=%async_computation.24 | async-start | bytes 4718592 | tf_op jit(solution)/shard_map/all_gather | solution.py:120
  381.0 141.1 %all-gather.12.cloned.1.call-start = ((), (), s32[]{:S(2)}) async-start(), calls=%async_computation.26 | async-start | bytes 4718592 | tf_op jit(solution)/shard_map/all_gather | solution.py:120
  383.9 279.2 %reduce-scatter.12.cloned.1.call-start = ((), (), s32[]{:S(2)}) async-start(), calls=%async_computation.27 | async-start | bytes 9437184 | tf_op jit(solution)/shard_map/reduce_scatter | solution.py:128
  551.0 185.8 %all-gather.14.cloned.1.call-start = ((), (), s32[]{:S(2)}) async-start(), calls=%async_computation.28 | async-start | bytes 4718592 | tf_op jit(solution)/shard_map/all_gather | solution.py:120
  667.1 211.5 %reduce-scatter.14.cloned.1.call-start = ((), (), s32[]{:S(2)}) async-start(), calls=%async_computation.29 | async-start | bytes 9437184 | tf_op jit(solution)/shard_map/reduce_scatter | solution.py:128
  747.0 13.1 %copy-start.16 = (bf16[2,128,1024]{2,1,0:T(8,128)(2,1)}, bf16[2,128,1024]{2,1,0:T(8,128)(2,1)S(1)}, u32[]{:S(2)}) copy-start(bf16[2,128,1024]{2,1,0:T(8,128)(2,1)S(1)} %fusion.36) | copy-start | bytes 1572868
  766.6 228.2 %reduce-scatter.10.cloned.1.call-start = ((), (), s32[]{:S(2)}) async-start(), calls=%async_computation.25 | async-start | bytes 9437184 | tf_op jit(solution)/shard_map/reduce_scatter | solution.py:128
  777.0 294.7 %reduce-scatter.16.cloned.1.call-start = ((), (), s32[]{:S(2)}) async-start(), calls=%async_computation.30 | async-start | bytes 11698176 | tf_op jit(solution)/shard_map/reduce_scatter | solution.py:29
  942.2 52.6 %copy-start.3 = (f32[128,2048]{1,0:T(8,128)S(1)}, f32[128,2048]{1,0:T(8,128)}, u32[]{:S(2)}) copy-start(f32[128,2048]{1,0:T(8,128)} %reduce-scatter.12.cloned.1.call-done) | copy-start | bytes 3145732
  1073.3 12.5 %all-to-all-start.8 = ((bf16[8,16,2]{1,2,0:T(2,128)(2,1)}), bf16[8,16,2]{1,2,0:T(2,128)(2,1)S(1)}, u32[]{:S(2)}, u32[]{:S(2)}) async-start(bf16[8,16,2]{1,2,0:T(2,128)(2,1)} %copy.111), calls=%async_computation.12 | async-start | bytes 8192 | tf_op jit(solution)/shard_map/all_to_all | solution.py:266
  1085.8 12.9 %all-to-all-start.9 = ((bf16[8,2,256]{2,1,0:T(2,128)(2,1)}), bf16[8,2,256]{2,1,0:T(2,128)(2,1)S(1)}, u32[]{:S(2)}, u32[]{:S(2)}) async-start(bf16[8,2,256]{2,1,0:T(2,128)(2,1)} %reshape.472), calls=%async_computation.13 | async-start | bytes 16384 | tf_op jit(solution)/shard_map/all_to_all | solution.py:245
  1098.7 9.8 all-to-all-start.10
  1108.5 9.9 all-to-all-start.12
  1118.4 9.9 all-to-all-start.11
  1128.3 10.4 all-to-all-start.13
  1138.7 10.8 all-to-all-start.15
  1149.5 10.6 all-to-all-start.14
  (24 other events, 100.6 us)
Sparse Core Ops, SparseCore 0:
  95.2 72.0 all-gather.5
  170.4 71.5 all-gather.7
  266.2 112.2 reduce-scatter.7
  381.1 69.4 all-gather.9
  452.7 69.3 all-gather.11
  551.1 112.0 reduce-scatter.11
  667.3 69.4 all-gather.13
  766.7 111.8 reduce-scatter.13
  882.5 112.2 reduce-scatter.9
  997.0 74.6 reduce-scatter.15
where the time goes:
time: 1190 us; the launch traced here: 1170 us
  waiting for transfers between devices  847 us (71%)
  matrix products  127 us (11%)
  local copies, waits for them, and re-layouts  92.5 us (8%)
  starting transfers between devices  65.5 us (6%)
  other arithmetic  20.4 us (2%)
  between operations  16.5 us (1%)
    reduce_scatter x4, waiting for transfers between devices, own_rows(): return lax.psum_scatter(total, 'seq', scatter_dimension=0, tiled=True)  356 us
    all_gather x4, waiting for transfers between devices, whole_row(): return lax.all_gather(piece, 'seq', axis=0, tiled=True)  261 us
    reduce_scatter x1, waiting for transfers between devices, sent_together(): lax.psum_scatter(both, axis, scatter_dimension=dim, tiled=True)  73.8 us
    all_gather x1, waiting for transfers between devices, side_by_side(): filled = lax.all_gather(both, axis, axis=dim, tiled=True)  71.9 us
    concatenate x1, local copies, waits for them, and re-layouts, sent_together(): both = jnp.concatenate(arrays, axis=along)  47.6 us
    dot_general x7, matrix products, contract_cols(): lax.dot_general(left, right, (((1,), (1,)), ((), ())), preferred_element_...  45.7 us
  transfers between devices with their start and end apart: 26, of which 26 were waited for; matrix products, arithmetic and copies ran while one was open for 12% of the time, Pallas kernels for 0%

commit v1 on v0

v1 whole, which is shorter than its diff:
```python
import math

import jax
import jax.numpy as jnp
import numpy as np
from jax import lax
from jax.sharding import Mesh, PartitionSpec as P

FEAT = 16
HEAD_V = 128
PAD_FF = 768
ATT_W = 640

norm_eps = 1e-05
AXES = ("zlo", "x", "core", "y", "zhi")
DP = ("zlo", "x", "core")
SEQ = ("y", "zhi")
TOKENS = ("y", "core")
COLUMNS = ("core", "y")
CHIPS = ("zhi", "zlo", "x")


def taylor(inputs):
    inner = inputs.shape[-1]
    lead = inputs.shape[:-1]
    first = inputs / inner**0.25
    second = (inputs[..., :, None] * inputs[..., None, :]).reshape(
        lead + (inner * inner,)
    ) / math.sqrt(2.0 * inner)
    return jnp.concatenate([jnp.ones(lead + (1,), jnp.float32), first, second], axis=-1)


def dot(left, right):
    return jnp.dot(left, right, preferred_element_type=jnp.float32)


def contract_rows(left, right):
    return lax.dot_general(
        left, right, (((0,), (0,)), ((), ())), preferred_element_type=jnp.float32
    )


def contract_cols(left, right):
    return lax.dot_general(
        left, right, (((1,), (1,)), ((), ())), preferred_element_type=jnp.float32
    )


def norm_back(grad_normed, inputs, inverse, gain):
    unit = inputs * inverse
    scaled = grad_normed * gain
    grad_gain = jnp.sum(grad_normed * unit, axis=0)
    grad_inputs = inverse * (scaled - unit * jnp.mean(scaled * unit, axis=-1, keepdims=True))
    return (grad_inputs, grad_gain)


def causal_mask(toks):
    return jnp.arange(toks)[:, None] >= jnp.arange(toks)[None, :]


def attend(feat_q, feat_k, values):
    causal = causal_mask(feat_q.shape[0])
    scores = jnp.einsum("thf,shf->hts", feat_q, feat_k, preferred_element_type=jnp.float32)
    scores = jnp.where(causal, scores, 0.0)
    numer = jnp.einsum("hts,shv->thv", scores, values.astype(jnp.float32))
    denom = jnp.sum(scores, axis=-1).T
    return (scores, denom, numer / denom[..., None])


def attend_back(grad_mixed, scores, denom, mixed, feat_q, feat_k, values):
    causal = causal_mask(feat_q.shape[0])
    grad_numer = grad_mixed / denom[..., None]
    grad_denom = -jnp.sum(grad_mixed * mixed, axis=-1) / denom
    query_wide = feat_q.astype(jnp.float32)
    key_wide = feat_k.astype(jnp.float32)
    values_wide = values.astype(jnp.float32)
    grad_scores = jnp.einsum("thv,shv->hts", grad_numer, values_wide)
    grad_scores = jnp.where(causal, grad_scores + grad_denom.T[..., None], 0.0)
    grad_feat_q = jnp.einsum("hts,shf->thf", grad_scores, key_wide)
    grad_feat_k = jnp.einsum("hts,thf->shf", grad_scores, query_wide)
    grad_values = jnp.einsum("hts,thv->shv", scores, grad_numer)
    return (grad_feat_q, grad_feat_k, grad_values)


def feature_back(query, keys, grad_feat_q, grad_feat_k, count):
    unused_q, pull_query = jax.vjp(taylor, query)
    grad_q = pull_query(grad_feat_q)[0].astype(jnp.bfloat16).reshape(count, -1)
    unused_k, pull_keys = jax.vjp(taylor, keys)
    grad_k = pull_keys(grad_feat_k)[0].astype(jnp.bfloat16).reshape(count, -1)
    return (grad_q, grad_k)


def row_scale(source_id, source_counts):
    picked = jnp.sum(
        jnp.where(
            source_id[:, None] == jnp.arange(source_counts.shape[0], dtype=jnp.int32)[None, :],
            source_counts[None, :],
            0,
        ),
        axis=1,
    )
    return 4.0 / jnp.sqrt(picked.astype(jnp.float32))


def lane_order(back):
    at = np.arange(256)
    to = (at // 16 % 2) * 128 + (at // 32) * 16 + at % 16
    hot = np.zeros((256, 256), np.float32)
    hot[at, to] = 1.0
    return jnp.asarray(hot.T if back else hot, jnp.bfloat16)


def reorder(array, hot, back):
    count, width = array.shape
    runs = width // 256
    if back:
        array = jnp.swapaxes(array.reshape(count, 2, runs, 128), 1, 2)
    moved = dot(array.reshape(count * runs, 256), hot).astype(jnp.bfloat16)
    if not back:
        moved = jnp.swapaxes(moved.reshape(count, runs, 2, 128), 1, 2)
    return moved.reshape(count, width)


def swap(array):
    return lax.ppermute(array, ("core", "zhi"), [(0, 0), (1, 2), (2, 1), (3, 3)])


def whole_row(piece):
    return lax.all_gather(piece, TOKENS, axis=0, tiled=True)


def own_rows(pairs):
    total = None
    for left, right in pairs:
        part = contract_cols(left, right)
        total = part if total is None else total + part
    return lax.psum_scatter(
        total.astype(jnp.bfloat16), TOKENS, scatter_dimension=0, tiled=True
    ).astype(jnp.float32)


def split_columns(weight, pad):
    rows, width = weight.shape
    cut = weight.reshape(rows, 8, width // 8)
    return jnp.pad(cut, ((0, 0), (0, 0), (0, pad)))


def body(
    hidden_in,
    norm1_gain,
    query_weight,
    key_weight,
    value_weight,
    out_weight,
    norm2_gain,
    gate_weight,
    up_weight,
    down_weight,
    cotangent,
    source_id,
    source_counts,
):
    rows, toks, width = hidden_in.shape
    ff_here = gate_weight.shape[1] // 8
    pad_ff = PAD_FF - ff_here
    depth = norm1_gain.shape[0]
    gains = jnp.stack((norm1_gain, norm2_gain), axis=1)[:, None, :]
    gains = jnp.broadcast_to(gains, (depth, 8, 2))
    pack_att = jnp.concatenate(
        (
            split_columns(value_weight, 0),
            split_columns(out_weight, 0),
            split_columns(query_weight, 0),
            split_columns(key_weight, 0),
            jnp.pad(gains, ((0, 0), (0, 0), (0, 62))),
        ),
        axis=2,
    )
    pack_mlp = jnp.concatenate(
        (
            split_columns(gate_weight, pad_ff),
            split_columns(up_weight, pad_ff),
            split_columns(down_weight, pad_ff),
        ),
        axis=2,
    )
    pack = jnp.swapaxes(jnp.concatenate((pack_att, pack_mlp), axis=2), 0, 1)
    pack = lax.all_to_all(pack, COLUMNS, split_axis=0, concat_axis=0, tiled=True)
    pack = pack.reshape(8 * depth, -1)
    att = lax.all_gather(pack[:, :ATT_W], CHIPS, axis=0, tiled=True)
    mlp = lax.all_gather(pack[:, ATT_W:], CHIPS, axis=0, tiled=True)
    w_value, w_out = att[:, :256], att[:, 256:512]
    w_query, w_key = att[:, 512:544], att[:, 544:576]
    norm1 = att[:, 576].astype(jnp.float32)
    norm2 = att[:, 577].astype(jnp.float32)
    w_gate, w_up, w_down = mlp[:, :PAD_FF], mlp[:, PAD_FF : 2 * PAD_FF], mlp[:, 2 * PAD_FF :]

    forth, back = lane_order(False), lane_order(True)
    raw = swap(reorder(hidden_in.reshape(toks, width), forth, False))
    scale = row_scale(source_id, source_counts)
    top = (cotangent.astype(jnp.float32) * scale[:, None, None]).reshape(toks, width)
    top_low = swap(reorder(top.astype(jnp.bfloat16), forth, False))
    grad_top = top_low.astype(jnp.float32)

    inputs = raw.astype(jnp.float32)
    inverse1 = lax.rsqrt(jnp.mean(inputs * inputs, axis=-1, keepdims=True) + norm_eps)
    normed = whole_row((inputs * inverse1 * norm1).astype(jnp.bfloat16))
    length = normed.shape[0]
    heads_here = w_query.shape[1] // FEAT
    query = dot(normed, w_query).reshape(length, heads_here, FEAT)
    keys = dot(normed, w_key).reshape(length, heads_here, FEAT)
    values = dot(normed, w_value).astype(jnp.bfloat16).reshape(length, heads_here, HEAD_V)
    feat_q = taylor(query).astype(jnp.bfloat16)
    feat_k = taylor(keys).astype(jnp.bfloat16)
    scores, denom, mixed = attend(feat_q, feat_k, values)
    attended = mixed.astype(jnp.bfloat16).reshape(length, heads_here * HEAD_V)
    middle = inputs + own_rows(((attended, w_out),))
    inverse2 = lax.rsqrt(jnp.mean(middle * middle, axis=-1, keepdims=True) + norm_eps)
    normed2 = whole_row((middle * inverse2 * norm2).astype(jnp.bfloat16))
    grad_low = whole_row(top_low)
    gate = dot(normed2, w_gate)
    upward = dot(normed2, w_up)
    sigma = jax.nn.sigmoid(gate)
    hidden = (gate * sigma * upward).astype(jnp.bfloat16)
    grad_down = contract_rows(grad_low, hidden).astype(jnp.bfloat16)
    grad_hidden = dot(grad_low, w_down)
    gate_act = (grad_hidden * upward * sigma * (1.0 + gate * (1.0 - sigma))).astype(jnp.bfloat16)
    up_act = (grad_hidden * gate * sigma).astype(jnp.bfloat16)
    grad_normed2 = own_rows(((gate_act, w_gate), (up_act, w_up)))
    layer_out = (middle + own_rows(((hidden, w_down),))).astype(jnp.bfloat16)
    grad_gate = contract_rows(normed2, gate_act).astype(jnp.bfloat16)
    grad_up = contract_rows(normed2, up_act).astype(jnp.bfloat16)
    grad_mid_norm, grad_norm2 = norm_back(grad_normed2, middle, inverse2, norm2)
    grad_middle = grad_top + grad_mid_norm
    middle_low = whole_row(grad_middle.astype(jnp.bfloat16))
    grads_mlp = lax.psum_scatter(
        jnp.concatenate((grad_gate, grad_up, grad_down), axis=1),
        CHIPS,
        scatter_dimension=0,
        tiled=True,
    )
    grad_out = contract_rows(middle_low, attended).astype(jnp.bfloat16)
    grad_mixed = dot(middle_low, w_out).reshape(length, heads_here, HEAD_V)
    grad_feat_q, grad_feat_k, grad_values = attend_back(
        grad_mixed, scores, denom, mixed, feat_q, feat_k, values
    )
    grad_values = grad_values.astype(jnp.bfloat16).reshape(length, heads_here * HEAD_V)
    grad_q, grad_k = feature_back(query, keys, grad_feat_q, grad_feat_k, length)
    grad_query = contract_rows(normed, grad_q).astype(jnp.bfloat16)
    grad_key = contract_rows(normed, grad_k).astype(jnp.bfloat16)
    grad_value = contract_rows(normed, grad_values).astype(jnp.bfloat16)
    grad_normed = own_rows(((grad_q, w_query), (grad_k, w_key), (grad_values, w_value)))
    grad_in_norm, grad_norm1 = norm_back(grad_normed, inputs, inverse1, norm1)
    grad_in = (grad_middle + grad_in_norm).astype(jnp.bfloat16)
    grad_pair = jnp.stack((grad_norm1, grad_norm2), axis=1).astype(jnp.bfloat16)
    grads_att = lax.psum_scatter(
        jnp.concatenate(
            (grad_value, grad_out, grad_query, grad_key, jnp.pad(grad_pair, ((0, 0), (0, 62)))),
            axis=1,
        ),
        CHIPS,
        scatter_dimension=0,
        tiled=True,
    )
    summed = jnp.concatenate((grads_att, grads_mlp), axis=1).reshape(8, depth, -1)
    summed = lax.all_to_all(summed, COLUMNS, split_axis=0, concat_axis=0, tiled=True)
    summed = jnp.swapaxes(summed, 0, 1).astype(jnp.float32)

    def joined(start, size):
        return summed[:, :, start : start + size].reshape(depth, 8 * size)

    pair = jnp.sum(summed[:, :, 576:578], axis=1)
    layer_out = reorder(swap(layer_out), back, True).reshape(rows, toks, width)
    grad_in = reorder(swap(grad_in), back, True).astype(jnp.float32).reshape(rows, toks, width)
    return (
        layer_out,
        grad_in,
        pair[:, 0],
        joined(512, 32),
        joined(544, 32),
        joined(0, 256),
        joined(256, 256),
        pair[:, 1],
        joined(ATT_W, ff_here),
        joined(ATT_W + PAD_FF, ff_here),
        joined(ATT_W + 2 * PAD_FF, ff_here),
    )


def solution(mesh):
    zlo, chips_x, cores, chips_y, zhi = 2, 4, 2, 4, 2
    whole = Mesh(mesh.devices.reshape(zlo, chips_x, cores, chips_y, zhi), AXES)
    weight = P(AXES, None)
    gain = P(AXES)
    tokens = P(DP, SEQ, None)
    return jax.shard_map(
        body,
        mesh=whole,
        in_specs=(
            tokens,
            gain,
            weight,
            weight,
            weight,
            weight,
            gain,
            weight,
            weight,
            weight,
            tokens,
            P(DP),
            P(),
        ),
        out_specs=(
            tokens,
            tokens,
            gain,
            weight,
            weight,
            weight,
            weight,
            gain,
            weight,
            weight,
            weight,
        ),
        check_vma=False,
    )
```

time: 1190 us -> 721 us (0.61); the launches traced: 1170 us -> 716 us
  waiting for transfers between devices: 847 us -> 472 us
  local copies, waits for them, and re-layouts: 92.5 us -> 44.5 us
  starting transfers between devices: 65.5 us -> 32.4 us
  matrix products: 127 us -> 105 us
  blocking collectives: 0 us -> 17.6 us
    reduce_scatter x5 -> x6, waiting for transfers between devices: 430 us -> 242 us  [the longest x4 83.7 us: own_rows(): lax.psum_scatter(total.astype(jnp.bfloat16), TOKENS, scatter_dimension=0,...]
    all_gather x5 -> x6, waiting for transfers between devices: 333 us -> 200 us  [the longest x4 116 us: whole_row(): return lax.all_gather(piece, TOKENS, axis=0, tiled=True)]
    all_to_all x16 -> x1, waiting for transfers between devices: 83.9 us -> 8.81 us  [body(): lax.all_to_all(summed, COLUMNS, split_axis=0, concat_axis=0, tiled=True)]
    all_to_all x16 -> x1, starting transfers between devices: 64.5 us -> 6.61 us  [body(): lax.all_to_all(summed, COLUMNS, split_axis=0, concat_axis=0, tiled=True)]
    concatenate x2 -> x1, local copies, waits for them, and re-layouts: 48.9 us -> 0.28 us  [body(): pack = jnp.swapaxes(jnp.concatenate((pack_att, pack_mlp), axis=2), 0, 1)]
    ppermute x0 -> x4, starting transfers between devices: none -> 24.2 us  [swap(): lax.ppermute(array, ('core', 'zhi'), [(0, 0), (1, 2), (2, 1), (3, 3)])]
    ppermute x0 -> x4, waiting for transfers between devices: none -> 21 us  [swap(): lax.ppermute(array, ('core', 'zhi'), [(0, 0), (1, 2), (2, 1), (3, 3)])]
    all_to_all x0 -> x1, blocking collectives: none -> 17.6 us  [body(): lax.all_to_all(pack, COLUMNS, split_axis=0, concat_axis=0, tiled=True)]
  transfers between devices with their start and end apart: 26 -> 17, of which waited for: 26 -> 14; matrix products, arithmetic and copies ran while one was open for 12% -> 12% of each run, Pallas kernels for 0% -> 0%
where the time goes in v1:
time: 721 us; the launch traced here: 716 us
  waiting for transfers between devices  472 us (65%)
  matrix products  105 us (15%)
  local copies, waits for them, and re-layouts  44.5 us (6%)
  starting transfers between devices  32.4 us (4%)
  other arithmetic  28.3 us (4%)
  blocking collectives  17.6 us (2%)
  between operations  16.6 us (2%)
    all_gather x4, waiting for transfers between devices, whole_row(): return lax.all_gather(piece, TOKENS, axis=0, tiled=True)  116 us
    reduce_scatter x4, waiting for transfers between devices, own_rows(): lax.psum_scatter(total.astype(jnp.bfloat16), TOKENS, scatter_dimension=0,...  83.7 us
    reduce_scatter x1, waiting for transfers between devices, body(): lax.psum_scatter(jnp.concatenate((grad_gate, grad_up, grad_down), axis=1)...  80.7 us
    reduce_scatter x1, waiting for transfers between devices, body(): lax.psum_scatter(jnp.concatenate((grad_value, grad_out, grad_query, grad_...  77.5 us
    all_gather x1, waiting for transfers between devices, body(): mlp = lax.all_gather(pack[:, ATT_W:], CHIPS, axis=0, tiled=True)  50.9 us
    dot_general x11, matrix products, dot(): return jnp.dot(left, right, preferred_element_type=jnp.float32)  37.8 us
    all_gather x1, waiting for transfers between devices, body(): att = lax.all_gather(pack[:, :ATT_W], CHIPS, axis=0, tiled=True)  32.9 us
    dot_general x7, matrix products, contract_cols(): lax.dot_general(left, right, (((1,), (1,)), ((), ())), preferred_element_...  30 us
  transfers between devices with their start and end apart: 17, of which 14 were waited for; matrix products, arithmetic and copies ran while one was open for 12% of the time, Pallas kernels for 0%

profile of v1, /device:TPU:1, one launch (start us, length us, event | category | flops | bytes accessed | tf_op | source)
XLA Modules:
  0.0 716.0 jit_solution(14357678530337583944)
XLA Ops:
  15.6 17.6 %all_to_all.10 = bf16[8,16,2944]{2,1,0:T(8,128)(2,1)S(1)} all-to-all(bf16[8,16,2944]{2,1,0:T(8,128)(2,1)S(1)} %copy.91), channel_id=1, replica_groups=mesh['zlo'=2,'x'=4,'core'=2,'y'=4,'zhi'=2] {'core','y'}, dimensions={0} | all-to-all | bytes 1507328 | tf_op jit(solution)/shard_map/all_to_all | solution.py:188
  35.8 5.8 collective-permute-start
  41.6 7.0 collective-permute-done
  48.8 32.9 %all-gather.7.cloned.1.call-done = bf16[2048,640]{1,0:T(8,128)(2,1)} async-done(((bf16[128,640]{1,0:T(8,128)(2,1)}), bf16[2048,640]{1,0:T(8,128)(2,1)}) %all-gather.7.cloned.1.call-update) | async-done | bytes 2621456 | tf_op jit(solution)/shard_map/all_gather | solution.py:190
  87.2 29.8 %all-gather.9.cloned.1.call-done = bf16[1024,2048]{1,0:T(8,128)(2,1)} async-done(((bf16[128,2048]{1,0:T(8,128)(2,1)}), bf16[1024,2048]{1,0:T(8,128)(2,1)}) %all-gather.9.cloned.1.call-update) | async-done | bytes 4194320 | tf_op jit(solution)/shard_map/all_gather | solution.py:129
  136.9 32.5 %reduce-scatter.11.cloned.1.call-done = bf16[128,2048]{1,0:T(8,128)(2,1)} async-done(((bf16[1024,2048]{1,0:T(8,128)(2,1)}), bf16[128,2048]{1,0:T(8,128)(2,1)}) %reduce-scatter.11.cloned.1.call-update) | async-done | bytes 524304 | tf_op jit(solution)/shard_map/reduce_scatter | solution.py:137
  175.6 8.3 %collective-permute-start.2 = (bf16[128,2048]{1,0:T(8,128)(2,1)S(1)}, bf16[128,2048]{1,0:T(8,128)(2,1)S(1)}, u32[]{:S(2)}, u32[]{:S(2)}) collective-permute-start(bf16[128,2048]{1,0:T(8,128)(2,1)S(1)} %bitcast.154), channel_id=1, source_target_pairs={{0,0},{1,8},{8,1},{9,9},{2,2},{3,10},{10,3},{11,11},{4,4},{5,12},{... | collective-permute-start | bytes 1572872 | tf_op jit(solution)/shard_map/ppermute | solution.py:125
  183.9 14.0 %collective-permute-done.2 = bf16[128,2048]{1,0:T(8,128)(2,1)S(1)} collective-permute-done((bf16[128,2048]{1,0:T(8,128)(2,1)S(1)}, bf16[128,2048]{1,0:T(8,128)(2,1)S(1)}, u32[]{:S(2)}, u32[]{:S(2)}) %collective-permute-start.2) | collective-permute-done | bytes 524320 | tf_op jit(solution)/shard_map/ppermute | solution.py:125
  199.0 50.9 %all-gather.13.cloned.1.call-done = bf16[2048,2304]{1,0:T(8,128)(2,1)} async-done(((bf16[128,2304]{1,0:T(8,128)(2,1)}), bf16[2048,2304]{1,0:T(8,128)(2,1)}) %all-gather.13.cloned.1.call-update) | async-done | bytes 9437200 | tf_op jit(solution)/shard_map/all_gather | solution.py:191
  249.8 33.7 %all-gather.11.cloned.1.call-done = bf16[1024,2048]{1,0:T(8,128)(2,1)} async-done(((bf16[128,2048]{1,0:T(8,128)(2,1)}), bf16[1024,2048]{1,0:T(8,128)(2,1)}) %all-gather.11.cloned.1.call-update) | async-done | bytes 4194320 | tf_op jit(solution)/shard_map/all_gather | solution.py:129
  283.6 8.3 %fusion.20 = f32[1024,768]{1,0:T(8,128)} fusion(bf16[1024,2048]{1,0:T(8,128)(2,1)} %all-gather.11.cloned.1.call-done, bf16[2048,2304]{1,0:T(8,128)(2,1)} %all-gather.13.cloned.1.call-done), kind=kOutput, calls=%fused_computation.35 | convolution fusion | flops 3221225472 | bytes 10485760 | tf_op jit(solution)/shard_map/dot_general | solution.py:34
  291.9 7.1 fusion.24
  299.0 18.2 %all-gather.15.cloned.1.call-done = bf16[1024,2048]{1,0:T(8,128)(2,1)} async-done(((bf16[128,2048]{1,0:T(8,128)(2,1)}), bf16[1024,2048]{1,0:T(8,128)(2,1)}) %all-gather.15.cloned.1.call-update) | async-done | bytes 4194320 | tf_op jit(solution)/shard_map/all_gather | solution.py:129
  317.2 10.5 %multiply_convert_fusion = (bf16[1024,768]{1,0:T(8,128)(2,1)S(1)}, bf16[1024,768]{1,0:T(8,128)(2,1)S(1)}, bf16[1024,768]{1,0:T(8,128)(2,1)}) fusion(f32[1024,768]{1,0:T(8,128)} %fusion.24, f32[1024,768]{1,0:T(8,128)} %fusion.20, bf16[1024,2048]{1,0:T(8,128)(2,1)} %all-gather.15.cloned.1.call-done, bf16[2048,2304]{1,0:T(8,128)(2,1)} %all-gather.13.cloned.1.call-done), kind=kOutput, calls=%fused_computation.27 | convolution fusion | flops 3233808384 | bytes 18350080 | tf_op jit(solution)/shard_map/dot_general | solution.py:34
  327.7 6.5 fusion.22
  334.2 6.9 add_convert_fusion.1
  341.2 34.5 %reduce-scatter.15.cloned.1.call-done = bf16[128,2048]{1,0:T(8,128)(2,1)} async-done(((bf16[1024,2048]{1,0:T(8,128)(2,1)}), bf16[128,2048]{1,0:T(8,128)(2,1)}) %reduce-scatter.15.cloned.1.call-update) | async-done | bytes 524304 | tf_op jit(solution)/shard_map/reduce_scatter | solution.py:137
  380.4 34.3 %all-gather.17.cloned.1.call-done = bf16[1024,2048]{1,0:T(8,128)(2,1)} async-done(((bf16[128,2048]{1,0:T(8,128)(2,1)}), bf16[1024,2048]{1,0:T(8,128)(2,1)}) %all-gather.17.cloned.1.call-update) | async-done | bytes 4194320 | tf_op jit(solution)/shard_map/all_gather | solution.py:129
  414.8 4.3 multiply_reduce_fusion.4
  437.9 6.9 convolution_convert_fusion.1
  444.9 6.1 convolution_convert_fusion.2
  454.9 3.9 convolution_convert_fusion.4
  458.8 4.3 pad_maximum_fusion
  463.1 12.5 %copy.117 = bf16[2048,2304]{1,0:T(8,128)(2,1)} copy(bf16[2048,2304]{0,1:T(8,128)(2,1)} %pad_maximum_fusion) | data formatting | bytes 18874368
  476.7 4.6 fusion.27
  488.8 4.5 copy.115
  493.4 16.7 %reduce-scatter.13.cloned.1.call-done = bf16[128,2048]{1,0:T(8,128)(2,1)} async-done(((bf16[1024,2048]{1,0:T(8,128)(2,1)}), bf16[128,2048]{1,0:T(8,128)(2,1)}) %reduce-scatter.13.cloned.1.call-update) | async-done | bytes 524304 | tf_op jit(solution)/shard_map/reduce_scatter | solution.py:137
  512.8 8.3 %collective-permute-start.3 = (bf16[128,2048]{1,0:T(8,128)(2,1)}, bf16[128,2048]{1,0:T(8,128)(2,1)S(1)}, u32[]{:S(2)}, u32[]{:S(2)}) collective-permute-start(bf16[128,2048]{1,0:T(8,128)(2,1)} %get-tuple-element.33), channel_id=1, source_target_pairs={{0,0},{1,8},{8,1},{9,9},{2,2},{3,10},{10,3},{11,11},{4,4},{5,12},{... | collective-permute-start | bytes 1572872 | tf_op jit(solution)/shard_map/ppermute | solution.py:125
  523.0 80.7 %reduce-scatter.21.cloned.1.call-done = bf16[128,2304]{1,0:T(8,128)(2,1)} async-done(((bf16[2048,2304]{1,0:T(8,128)(2,1)}), bf16[128,2304]{1,0:T(8,128)(2,1)}) %reduce-scatter.21.cloned.1.call-update) | async-done | bytes 589840 | tf_op jit(solution)/shard_map/reduce_scatter | solution.py:236
  603.7 77.5 %reduce-scatter.19.cloned.1.call-done = bf16[128,640]{1,0:T(8,128)(2,1)} async-done(((bf16[2048,640]{1,0:T(8,128)(2,1)}), bf16[128,640]{1,0:T(8,128)(2,1)}) %reduce-scatter.19.cloned.1.call-update) | async-done | bytes 163856 | tf_op jit(solution)/shard_map/reduce_scatter | solution.py:256
  683.2 6.6 all-to-all-start.1
  692.8 8.8 %all-to-all-done.1 = bf16[8,16,2944]{2,1,0:T(8,128)(2,1)S(1)} async-done(((bf16[8,16,2944]{2,1,0:T(8,128)(2,1)}), bf16[8,16,2944]{2,1,0:T(8,128)(2,1)S(1)}, u32[]{:S(2)}, u32[]{:S(2)}) %all-to-all-start.1) | async-done | bytes 753696 | tf_op jit(solution)/shard_map/all_to_all | solution.py:266
  (230 shorter events, 95.0 us)
Async XLA Ops:
  7.2 74.5 %all-gather.7.cloned.1.call-start = ((), (), s32[]{:S(2)}) async-start(), calls=%async_computation.8 | async-start | bytes 2785280 | tf_op jit(solution)/shard_map/all_gather | solution.py:190
  13.8 21.0 %copy-start.24 = (bf16[1,128,2048]{2,1,0:T(8,128)(2,1)S(1)}, bf16[1,128,2048]{2,1,0:T(8,128)(2,1)}, u32[]{:S(2)}) copy-start(bf16[1,128,2048]{2,1,0:T(8,128)(2,1)} %param.15) | copy-start | bytes 1572868
  34.8 82.3 %all-gather.9.cloned.1.call-start = ((), (), s32[]{:S(2)}) async-start(), calls=%async_computation.9 | async-start | bytes 4718592 | tf_op jit(solution)/shard_map/all_gather | solution.py:129
  35.8 12.8 %collective-permute-start = (bf16[128,2048]{1,0:T(8,128)(2,1)S(1)}, bf16[128,2048]{1,0:T(8,128)(2,1)S(1)}, u32[]{:S(2)}, u32[]{:S(2)}) collective-permute-start(bf16[128,2048]{1,0:T(8,128)(2,1)S(1)} %bitcast.153), channel_id=1, source_target_pairs={{0,0},{1,8},{8,1},{9,9},{2,2},{3,10},{10,3},{11,11},{4,4},{5,12},{... | collective-permute-start | bytes 1572872 | tf_op jit(solution)/shard_map/ppermute | solution.py:125
  48.8 71.9 %copy-start.36 = (f32[128]{0:T(128)}, f32[128]{0:T(128)S(1)}, u32[]{:S(2)}) copy-start(f32[128]{0:T(128)S(1)} %add_rsqrt_fusion.1) | copy-start | bytes 1540
  81.7 35.4 %copy-start.3 = (bf16[2048,640]{1,0:T(8,128)(2,1)S(1)}, bf16[2048,640]{1,0:T(8,128)(2,1)}, u32[]{:S(2)}) copy-start(bf16[2048,640]{1,0:T(8,128)(2,1)} %all-gather.7.cloned.1.call-done) | copy-start | bytes 7864324
  83.8 37.0 %copy-start.27 = (f32[2048]{0:T(1024)}, f32[2048]{0:T(1024)S(1)}, u32[]{:S(2)}) copy-start(f32[2048]{0:T(1024)S(1)} %get-tuple-element.12) | copy-start | bytes 24580
  84.8 84.6 %reduce-scatter.11.cloned.1.call-start = ((), (), s32[]{:S(2)}) async-start(), calls=%async_computation.10 | async-start | bytes 4718592 | tf_op jit(solution)/shard_map/reduce_scatter | solution.py:137
  134.9 38.6 %copy-start.45 = (s32[8]{0:T(128)S(1)}, s32[8]{0:T(128)}, u32[]{:S(2)}) copy-start(s32[8]{0:T(128)} %param.27) | copy-start | bytes 100
  134.9 39.9 %copy-start.25 = (bf16[1,128,2048]{2,1,0:T(8,128)(2,1)S(1)}, bf16[1,128,2048]{2,1,0:T(8,128)(2,1)}, u32[]{:S(2)}) copy-start(bf16[1,128,2048]{2,1,0:T(8,128)(2,1)} %param.25) | copy-start | bytes 1572868
  134.9 114.9 %all-gather.13.cloned.1.call-start = ((), (), s32[]{:S(2)}) async-start(), calls=%async_computation.12 | async-start | bytes 10027008 | tf_op jit(solution)/shard_map/all_gather | solution.py:191
  136.8 146.7 %all-gather.11.cloned.1.call-start = ((), (), s32[]{:S(2)}) async-start(), calls=%async_computation.11 | async-start | bytes 4718592 | tf_op jit(solution)/shard_map/all_gather | solution.py:129
  170.7 207.1 %copy-start.34 = (f32[128]{0:T(128)}, f32[128]{0:T(128)S(1)}, u32[]{:S(2)}) copy-start(f32[128]{0:T(128)S(1)} %add_rsqrt_fusion) | copy-start | bytes 1540
  172.8 144.4 %all-gather.15.cloned.1.call-start = ((), (), s32[]{:S(2)}) async-start(), calls=%async_computation.14 | async-start | bytes 4718592 | tf_op jit(solution)/shard_map/all_gather | solution.py:129
  175.6 22.3 %collective-permute-start.2 = (bf16[128,2048]{1,0:T(8,128)(2,1)S(1)}, bf16[128,2048]{1,0:T(8,128)(2,1)S(1)}, u32[]{:S(2)}, u32[]{:S(2)}) collective-permute-start(bf16[128,2048]{1,0:T(8,128)(2,1)S(1)} %bitcast.154), channel_id=1, source_target_pairs={{0,0},{1,8},{8,1},{9,9},{2,2},{3,10},{10,3},{11,11},{4,4},{5,12},{... | collective-permute-start | bytes 1572872 | tf_op jit(solution)/shard_map/ppermute | solution.py:125
  198.7 176.9 %reduce-scatter.15.cloned.1.call-start = ((), (), s32[]{:S(2)}) async-start(), calls=%async_computation.15 | async-start | bytes 4718592 | tf_op jit(solution)/shard_map/reduce_scatter | solution.py:137
  341.1 34.6 %copy-start.2 = (bf16[128,2048]{1,0:T(8,128)(2,1)S(1)}, bf16[128,2048]{1,0:T(8,128)(2,1)}, u32[]{:S(2)}) copy-start(bf16[128,2048]{1,0:T(8,128)(2,1)} %reduce-scatter.11.cloned.1.call-done) | copy-start | bytes 1572868
  341.1 36.7 %copy-start.6 = (bf16[128,2048]{1,0:T(8,128)(2,1)S(1)}, bf16[128,2048]{1,0:T(8,128)(2,1)}, u32[]{:S(2)}) copy-start(bf16[128,2048]{1,0:T(8,128)(2,1)} %copy-done.5) | copy-start | bytes 1572868
  341.1 73.6 %all-gather.17.cloned.1.call-start = ((), (), s32[]{:S(2)}) async-start(), calls=%async_computation.16 | async-start | bytes 4718592 | tf_op jit(solution)/shard_map/all_gather | solution.py:129
  377.8 36.9 %copy-start.38 = (f32[128]{0:T(128)}, f32[128]{0:T(128)S(1)}, u32[]{:S(2)}) copy-start(f32[128]{0:T(128)S(1)} %broadcast_multiply_fusion.1) | copy-start | bytes 1540
  380.2 106.4 %reduce-scatter.17.cloned.1.call-start = ((), (), s32[]{:S(2)}) async-start(), calls=%async_computation.17 | async-start | bytes 4718592 | tf_op jit(solution)/shard_map/reduce_scatter | solution.py:137
  436.5 73.6 %reduce-scatter.13.cloned.1.call-start = ((), (), s32[]{:S(2)}) async-start(), calls=%async_computation.13 | async-start | bytes 4718592 | tf_op jit(solution)/shard_map/reduce_scatter | solution.py:137
  444.8 158.9 %reduce-scatter.21.cloned.1.call-start = ((), (), s32[]{:S(2)}) async-start(), calls=%async_computation.19 | async-start | bytes 10027008 | tf_op jit(solution)/shard_map/reduce_scatter | solution.py:236
  475.6 205.5 %reduce-scatter.19.cloned.1.call-start = ((), (), s32[]{:S(2)}) async-start(), calls=%async_computation.18 | async-start | bytes 2785280 | tf_op jit(solution)/shard_map/reduce_scatter | solution.py:256
  488.8 21.3 %copy-start.7 = (bf16[128,2048]{1,0:T(8,128)(2,1)S(1)}, bf16[128,2048]{1,0:T(8,128)(2,1)}, u32[]{:S(2)}) copy-start(bf16[128,2048]{1,0:T(8,128)(2,1)} %reduce-scatter.15.cloned.1.call-done) | copy-start | bytes 1572868
  488.8 21.3 %copy-start.10 = (bf16[128,2048]{1,0:T(8,128)(2,1)S(1)}, bf16[128,2048]{1,0:T(8,128)(2,1)}, u32[]{:S(2)}) copy-start(bf16[128,2048]{1,0:T(8,128)(2,1)} %reduce-scatter.17.cloned.1.call-done) | copy-start | bytes 1572868
  488.8 21.3 %copy-start.35 = (f32[128]{0:T(128)S(1)}, f32[128]{0:T(128)}, u32[]{:S(2)}) copy-start(f32[128]{0:T(128)} %copy-done.34) | copy-start | bytes 1540
  488.8 21.3 %copy-start.39 = (f32[128]{0:T(128)S(1)}, f32[128]{0:T(128)}, u32[]{:S(2)}) copy-start(f32[128]{0:T(128)} %copy-done.38) | copy-start | bytes 1540
  493.4 196.5 %copy-start.26 = (bf16[256,256]{1,0:T(8,128)(2,1)S(1)}, bf16[256,256]{1,0:T(8,128)(2,1)}, u32[]{:S(2)}) copy-start(bf16[256,256]{1,0:T(8,128)(2,1)} %constant.39.clone) | copy-start | bytes 393220
  512.8 177.0 %collective-permute-start.3 = (bf16[128,2048]{1,0:T(8,128)(2,1)}, bf16[128,2048]{1,0:T(8,128)(2,1)S(1)}, u32[]{:S(2)}, u32[]{:S(2)}) collective-permute-start(bf16[128,2048]{1,0:T(8,128)(2,1)} %get-tuple-element.33), channel_id=1, source_target_pairs={{0,0},{1,8},{8,1},{9,9},{2,2},{3,10},{10,3},{11,11},{4,4},{5,12},{... | collective-permute-start | bytes 1572872 | tf_op jit(solution)/shard_map/ppermute | solution.py:125
  521.1 170.3 %collective-permute-start.1 = (bf16[128,2048]{1,0:T(8,128)(2,1)S(1)}, bf16[128,2048]{1,0:T(8,128)(2,1)S(1)}, u32[]{:S(2)}, u32[]{:S(2)}) collective-permute-start(bf16[128,2048]{1,0:T(8,128)(2,1)S(1)} %get-tuple-element.34), channel_id=1, source_target_pairs={{0,0},{1,8},{8,1},{9,9},{2,2},{3,10},{10,3},{11,11},{4,4},{5,12},{... | collective-permute-start | bytes 1572872 | tf_op jit(solution)/shard_map/ppermute | solution.py:125
  683.2 18.4 %all-to-all-start.1 = ((bf16[8,16,2944]{2,1,0:T(8,128)(2,1)}), bf16[8,16,2944]{2,1,0:T(8,128)(2,1)S(1)}, u32[]{:S(2)}, u32[]{:S(2)}) async-start(bf16[8,16,2944]{2,1,0:T(8,128)(2,1)} %bitcast.33), calls=%async_computation.5 | async-start | bytes 1507328 | tf_op jit(solution)/shard_map/all_to_all | solution.py:266
  (38 other events, 138.3 us)
Sparse Core Ops, SparseCore 0:
  34.9 46.7 all-gather.6
  84.9 32.0 all-gather.8
  135.0 34.3 reduce-scatter.10
  171.4 78.3 all-gather.12
  251.4 32.1 all-gather.10
  285.1 32.0 all-gather.14
  341.3 34.3 reduce-scatter.14
  380.3 34.4 all-gather.16
  436.7 34.3 reduce-scatter.16
  473.3 36.7 reduce-scatter.12
  513.6 90.0 reduce-scatter.20
  607.2 73.8 reduce-scatter.18

commit v2 on v1

--- a/solution.py
+++ b/solution.py
@@ -4,6 +4,8 @@
 import jax.numpy as jnp
 import numpy as np
 from jax import lax
+from jax.experimental import pallas as pl
+from jax.experimental.pallas import tpu as pltpu
 from jax.sharding import Mesh, PartitionSpec as P
 
 FEAT = 16
@@ -44,14 +46,6 @@
     return lax.dot_general(
         left, right, (((1,), (1,)), ((), ())), preferred_element_type=jnp.float32
     )
-
-
-def norm_back(grad_normed, inputs, inverse, gain):
-    unit = inputs * inverse
-    scaled = grad_normed * gain
-    grad_gain = jnp.sum(grad_normed * unit, axis=0)
-    grad_inputs = inverse * (scaled - unit * jnp.mean(scaled * unit, axis=-1, keepdims=True))
-    return (grad_inputs, grad_gain)
 
 
 def causal_mask(toks):
@@ -137,6 +131,572 @@
     return lax.psum_scatter(
         total.astype(jnp.bfloat16), TOKENS, scatter_dimension=0, tiled=True
     ).astype(jnp.float32)
+
+
+MESH = pl.DeviceIdType.MESH
+VMEM_LIMIT = 52 * 2**20
+PIECES = 4
+TILE = 256
+
+
+def place():
+    z = lax.axis_index("zhi") * 2 + lax.axis_index("zlo")
+    return lax.axis_index("x"), lax.axis_index("y"), z, lax.axis_index("core")
+
+
+def at_y(y):
+    return {"y": lax.rem(y + 8, 4)}
+
+
+def at_core(core):
+    return {"core": core}
+
+
+def at_xz(x, z):
+    x, z = lax.rem(x + 8, 4), lax.rem(z + 8, 4)
+    return {"x": x, "zhi": z // 2, "zlo": lax.rem(z, 2)}
+
+
+def greet(devices):
+    barrier = pltpu.get_barrier_semaphore()
+    for device in devices:
+        pl.semaphore_signal(barrier, inc=1, device_id=device, device_id_type=MESH)
+    pl.semaphore_wait(barrier, len(devices))
+
+
+class Copies:
+    def __init__(self, send, recv):
+        self.send, self.recv, self.used, self.open = send, recv, 0, []
+
+    def start(self, src, dst, device):
+        copy = pltpu.make_async_remote_copy(
+            src_ref=src,
+            dst_ref=dst,
+            send_sem=self.send.at[self.used],
+            recv_sem=self.recv.at[self.used],
+            device_id=device,
+            device_id_type=MESH,
+        )
+        copy.start()
+        self.used += 1
+        self.open.append(copy)
+        return copy
+
+    def local(self, src, dst):
+        copy = pltpu.make_async_copy(src, dst, self.send.at[self.used])
+        copy.start()
+        self.used += 1
+        return copy
+
+    def finish(self):
+        for copy in self.open:
+            copy.wait_send()
+
+
+def way(piece):
+    return 1 if piece % 2 == 0 else -1
+
+
+def rows_of(piece, rows):
+    size = rows // PIECES
+    return pl.ds(piece * size, size)
+
+
+def gather_ring(copies, to, mine, full, block_of, me, rows):
+    sent = {}
+    for piece in range(PIECES):
+        for step in (way(piece), -way(piece)):
+            part = rows_of(piece, rows)
+            sent[step, piece] = copies.start(
+                mine.at[part], full.at[block_of(me), part], to(me + step)
+            )
+    onward = {}
+
+    def forward():
+        for piece in range(PIECES):
+            step = way(piece)
+            sent[step, piece].wait_recv()
+            here = full.at[block_of(me - step), rows_of(piece, rows)]
+            onward[piece] = copies.start(here, here, to(me + step))
+
+    def near():
+        for piece in range(PIECES):
+            sent[-way(piece), piece].wait_recv()
+
+    def far():
+        for piece in range(PIECES):
+            onward[piece].wait_recv()
+
+    return forward, near, far
+
+
+def gather_tokens(copies, mine, full, y, core):
+    rows = mine.shape[0]
+    other = at_core(1 - core)
+
+    def block_of(index):
+        return lax.rem(index + 8, 4) * 2 + core
+
+    own = copies.local(mine, full.at[block_of(y)])
+    shared = [copies.start(mine, full.at[block_of(y)], other)]
+    forward, near, far = gather_ring(copies, at_y, mine, full, block_of, y, rows)
+
+    def finish():
+        forward()
+        near()
+        for step in (1, -1):
+            here = full.at[block_of(y + step)]
+            shared.append(copies.start(here, here, other))
+        far()
+        here = full.at[block_of(y + 2)]
+        shared.append(copies.start(here, here, other))
+        for copy in shared:
+            copy.wait_recv()
+        own.wait()
+
+    return finish
+
+
+def gather_plane(copies, mine, full, x, z, core):
+    rows = mine.shape[0]
+
+    def block(a, b):
+        a, b = lax.rem(a + 8, 4), lax.rem(b + 8, 4)
+        return jnp.where(core == 0, 4 * b + a, 4 * a + b)
+
+    first, second = jnp.where(core == 0, x, z), jnp.where(core == 0, z, x)
+
+    def to_first(index):
+        return at_xz(jnp.where(core == 0, index, x), jnp.where(core == 0, z, index))
+
+    def to_second(index):
+        return at_xz(jnp.where(core == 0, x, index), jnp.where(core == 0, index, z))
+
+    own = copies.local(mine, full.at[block(first, second)])
+    forward, near, far = gather_ring(
+        copies, to_first, mine, full, lambda a: block(a, second), first, rows
+    )
+
+    def onto_second(a, source):
+        return gather_ring(
+            copies, to_second, source, full, lambda b: block(a, b), second, rows
+        )
+
+    def finish():
+        rings = [onto_second(first, mine)]
+        forward()
+        near()
+        for step in (1, -1):
+            rings.append(onto_second(first + step, full.at[block(first + step, second)]))
+        rings[0][0]()
+        far()
+        rings.append(onto_second(first + 2, full.at[block(first + 2, second)]))
+        for ring in rings[1:]:
+            ring[0]()
+        for ring in rings:
+            ring[1]()
+            ring[2]()
+        own.wait()
+
+    return finish
+
+
+def reduce_ring(copies, to, me, part, out, got, rows, step_rows=16):
+    size = rows // PIECES
+
+    def each(piece, act):
+        @pl.loop(0, size // step_rows)
+        def _(at):
+            act(pl.ds(piece * size + at * step_rows, step_rows))
+
+    sent = {}
+    for piece in range(PIECES):
+        step = way(piece)
+        span = rows_of(piece, rows)
+
+        def far(span):
+            out[0, span] = part(2, span).astype(jnp.bfloat16)
+
+        each(piece, far)
+        sent[0, piece] = copies.start(out.at[0, span], got.at[0, span], to(me + step))
+    for piece in range(PIECES):
+        step = way(piece)
+        span = rows_of(piece, rows)
+
+        def near(span):
+            out[1, span] = part(-step, span).astype(jnp.bfloat16)
+
+        each(piece, near)
+        sent[1, piece] = copies.start(out.at[1, span], got.at[1, span], to(me - step))
+    for piece in range(PIECES):
+        step = way(piece)
+        span = rows_of(piece, rows)
+        sent[0, piece].wait_recv()
+
+        def onward(span):
+            out[2, span] = (part(step, span) + got[0, span].astype(jnp.float32)).astype(jnp.bfloat16)
+
+        each(piece, onward)
+        sent[2, piece] = copies.start(out.at[2, span], got.at[2, span], to(me + step))
+
+    def arrive(piece):
+        sent[1, piece].wait_recv()
+        sent[2, piece].wait_recv()
+
+    def total(span):
+        return part(0, span) + got[1, span].astype(jnp.float32) + got[2, span].astype(jnp.float32)
+
+    return arrive, total
+
+
+def spread_kernel(att, mlp, raw, top, att_out, mlp_out, raw_out, top_out, send, recv):
+    unused_x, y, z, core = place()
+    zhi = z // 2
+    copies = Copies(send, recv)
+    others = [(dc, dy) for dc in (0, 1) for dy in range(4) if (dc, dy) != (0, 0)]
+
+    def there(dc, dy):
+        return lax.rem(core + dc, 2), lax.rem(y + dy, 4)
+
+    barrier = pltpu.get_barrier_semaphore()
+    for dc, dy in others:
+        to_core, to_y = there(dc, dy)
+        pl.semaphore_signal(barrier, inc=1, device_id={"core": to_core, "y": to_y}, device_id_type=MESH)
+    partner = {"core": 1 - core, "zhi": 1 - zhi}
+
+    @pl.when(core != zhi)
+    def _():
+        pl.semaphore_signal(barrier, inc=1, device_id=partner, device_id_type=MESH)
+
+    pl.semaphore_wait(barrier, len(others) + jnp.where(core != zhi, 1, 0))
+    me = core * 4 + y
+    local = [copies.local(att.at[me], att_out.at[me]), copies.local(mlp.at[me], mlp_out.at[me])]
+    pairs = ((raw, raw_out), (top, top_out))
+    sems = []
+    for _ in pairs:
+        sems.append(copies.used)
+        copies.used += 1
+
+    def over(pair, sem):
+        return pltpu.make_async_remote_copy(
+            src_ref=pair[0],
+            dst_ref=pair[1],
+            send_sem=send.at[sem],
+            recv_sem=recv.at[sem],
+            device_id=partner,
+            device_id_type=MESH,
+        )
+
+    def stay(pair, sem):
+        return pltpu.make_async_copy(pair[0], pair[1], send.at[sem])
+
+    @pl.when(core != zhi)
+    def _():
+        for pair, sem in zip(pairs, sems):
+            over(pair, sem).start()
+
+    @pl.when(core == zhi)
+    def _():
+        for pair, sem in zip(pairs, sems):
+            stay(pair, sem).start()
+
+    for dc, dy in others:
+        to_core, to_y = there(dc, dy)
+        to = {"core": to_core, "y": to_y}
+        copies.start(att.at[to_core * 4 + to_y], att_out.at[me], to)
+        copies.start(mlp.at[to_core * 4 + to_y], mlp_out.at[me], to)
+    for copy in copies.open:
+        copy.wait_recv()
+    copies.finish()
+    for copy in local:
+        copy.wait()
+
+    @pl.when(core != zhi)
+    def _():
+        for pair, sem in zip(pairs, sems):
+            over(pair, sem).wait()
+
+    @pl.when(core == zhi)
+    def _():
+        for pair, sem in zip(pairs, sems):
+            stay(pair, sem).wait()
+
+
+def first_kernel(raw, att, raw_full, att_full, send, recv):
+    x, y, z, core = place()
+    greet(
+        [at_y(y + 1), at_y(y - 1), at_core(1 - core)]
+        + [at_xz(x + 1, z), at_xz(x - 1, z), at_xz(x, z + 1), at_xz(x, z - 1)]
+    )
+    copies = Copies(send, recv)
+    tokens = gather_tokens(copies, raw, raw_full, y, core)
+    plane = gather_plane(copies, att, att_full, x, z, core)
+    tokens()
+    plane()
+    copies.finish()
+
+
+def tile_parts(lefts, rights, block, core, mine, theirs):
+    rows = pl.ds(pl.multiple_of(block * 256, 256), 256)
+
+    @pl.loop(0, mine.shape[-1] // TILE)
+    def _(tile):
+        columns = pl.ds(pl.multiple_of(tile * TILE, TILE), TILE)
+        total = None
+        for left, (right, lanes) in zip(lefts, rights):
+            term = lax.dot_general(
+                left[rows, :],
+                right[columns, lanes],
+                (((1,), (1,)), ((), ())),
+                preferred_element_type=jnp.float32,
+            )
+            total = term if total is None else total + term
+        low, high = total[:128], total[128:]
+        mine[:, columns] = jnp.where(core == 0, low, high)
+        theirs[:, columns] = jnp.where(core == 0, high, low).astype(jnp.bfloat16)
+
+
+def reduce_tokens(copies, lefts, rights, y, core, own, sib, got_sib, out, got):
+    shared = {}
+    for k in (2, 1, 3, 0):
+        tile_parts(lefts, rights, lax.rem(y + k, 4), core, own.at[k], sib.at[k])
+        shared[k] = copies.start(sib.at[k], got_sib.at[k], at_core(1 - core))
+    for k in (2, 1, 3, 0):
+        shared[k].wait_recv()
+
+    def part(k, span):
+        k = k % 4
+        return own[k, span] + got_sib[k, span].astype(jnp.float32)
+
+    return reduce_ring(copies, at_y, y, part, out, got, own.shape[1])
+
+
+def greet_tokens(y, core):
+    greet([at_y(y + 1), at_y(y - 1), at_core(1 - core)])
+
+
+def middle_kernel(
+    attended, att, raw, gain, middle, normed2, own, sib, got_sib, out, got, low, send, recv
+):
+    unused_x, y, unused_z, core = place()
+    greet_tokens(y, core)
+    copies = Copies(send, recv)
+    arrive, total = reduce_tokens(
+        copies, [attended], [(att, slice(256, 512))], y, core, own, sib, got_sib, out, got
+    )
+    for piece in range(PIECES):
+        arrive(piece)
+
+    @pl.loop(0, 128 // 16)
+    def _(at):
+        span = pl.ds(at * 16, 16)
+        value = raw[span].astype(jnp.float32) + total(span)
+        middle[span] = value
+        inverse = lax.rsqrt(jnp.mean(value * value, axis=-1, keepdims=True) + norm_eps)
+        low[span] = (value * inverse * gain[...]).astype(jnp.bfloat16)
+
+    finish = gather_tokens(copies, low, normed2, y, core)
+    finish()
+    copies.finish()
+
+
+def norm_back_rows(grad, value, gain):
+    inverse = lax.rsqrt(jnp.mean(value * value, axis=-1, keepdims=True) + norm_eps)
+    unit = value * inverse
+    scaled = grad * gain
+    moved = inverse * (scaled - unit * jnp.mean(scaled * unit, axis=-1, keepdims=True))
+    return moved, grad * unit
+
+
+def eight(terms):
+    return terms[:8] + terms[8:]
+
+
+def middle_back_kernel(
+    gate_act,
+    up_act,
+    mlp,
+    middle,
+    top,
+    gain,
+    grad_middle,
+    grad_gain,
+    middle_low,
+    own,
+    sib,
+    got_sib,
+    out,
+    got,
+    low,
+    send,
+    recv,
+):
+    unused_x, y, unused_z, core = place()
+    greet_tokens(y, core)
+    copies = Copies(send, recv)
+    arrive, total = reduce_tokens(
+        copies,
+        [gate_act, up_act],
+        [(mlp, slice(0, PAD_FF)), (mlp, slice(PAD_FF, 2 * PAD_FF))],
+        y,
+        core,
+        own,
+        sib,
+        got_sib,
+        out,
+        got,
+    )
+    for piece in range(PIECES):
+        arrive(piece)
+    grad_gain[...] = jnp.zeros_like(grad_gain)
+
+    @pl.loop(0, 128 // 16)
+    def _(at):
+        span = pl.ds(at * 16, 16)
+        moved, terms = norm_back_rows(total(span), middle[span], gain[...])
+        grad_gain[...] += eight(terms)
+        value = top[span].astype(jnp.float32) + moved
+        grad_middle[span] = value
+        low[span] = value.astype(jnp.bfloat16)
+
+    finish = gather_tokens(copies, low, middle_low, y, core)
+    finish()
+    copies.finish()
+
+
+def input_back_kernel(
+    grad_qk, grad_values, att, raw, grad_middle, gain, grad_in, grad_gain, own, sib, got_sib, out, got, send, recv
+):
+    unused_x, y, unused_z, core = place()
+    greet_tokens(y, core)
+    copies = Copies(send, recv)
+    arrive, total = reduce_tokens(
+        copies,
+        [grad_values, grad_qk],
+        [(att, slice(0, 256)), (att, slice(512, 640))],
+        y,
+        core,
+        own,
+        sib,
+        got_sib,
+        out,
+        got,
+    )
+    for piece in range(PIECES):
+        arrive(piece)
+    grad_gain[...] = jnp.zeros_like(grad_gain)
+
+    @pl.loop(0, 128 // 16)
+    def _(at):
+        span = pl.ds(at * 16, 16)
+        moved, terms = norm_back_rows(total(span), raw[span].astype(jnp.float32), gain[...])
+        grad_gain[...] += eight(terms)
+        grad_in[span] = (grad_middle[span] + moved).astype(jnp.bfloat16)
+
+    copies.finish()
+
+
+def reduce_plane(copies, parts, x, z, core, out1, got1, mid, out2, got2):
+    rows = parts.shape[1]
+
+    def block(a, b):
+        a, b = lax.rem(a + 8, 4), lax.rem(b + 8, 4)
+        return jnp.where(core == 0, 4 * b + a, 4 * a + b)
+
+    last, first = jnp.where(core == 0, x, z), jnp.where(core == 0, z, x)
+
+    def to_last(index):
+        return at_xz(jnp.where(core == 0, index, x), jnp.where(core == 0, z, index))
+
+    def to_first(index):
+        return at_xz(jnp.where(core == 0, x, index), jnp.where(core == 0, index, z))
+
+    rings = {}
+    for k in (2, 1, 3, 0):
+
+        def part(step, span, k=k):
+            return parts[block(last + k, first + step), span].astype(jnp.float32)
+
+        rings[k] = reduce_ring(copies, to_first, first, part, out1.at[k], got1.at[k], rows, rows // PIECES)
+    for k in (2, 1, 3, 0):
+        arrive, total = rings[k]
+        for piece in range(PIECES):
+            arrive(piece)
+            span = rows_of(piece, rows)
+            mid[k, span] = total(span)
+
+    def part2(step, span):
+        return mid[step % 4, span]
+
+    return reduce_ring(copies, to_last, last, part2, out2, got2, rows, rows // PIECES)
+
+
+def last_kernel(
+    att, mlp, att_out, mlp_out, out1, got1, mid, out2, got2, summed, send, recv
+):
+    x, y, z, core = place()
+    others = [(dc, dy) for dc in (0, 1) for dy in range(4) if (dc, dy) != (0, 0)]
+
+    def there(dc, dy):
+        return lax.rem(core + dc, 2), lax.rem(y + dy, 4)
+
+    greet(
+        [{"core": there(dc, dy)[0], "y": there(dc, dy)[1]} for dc, dy in others]
+        + [at_xz(x + 1, z), at_xz(x - 1, z), at_xz(x, z + 1), at_xz(x, z - 1)]
+    )
+    copies = Copies(send, recv)
+    me = core * 4 + y
+    local = [copies.local(mlp.at[me], mlp_out.at[me])]
+    back = []
+    for dc, dy in others:
+        to_core, to_y = there(dc, dy)
+        to = {"core": to_core, "y": to_y}
+        back.append(copies.start(mlp.at[to_core * 4 + to_y], mlp_out.at[me], to))
+    arrive, total = reduce_plane(copies, att, x, z, core, out1, got1, mid, out2, got2)
+    size = summed.shape[0] * summed.shape[1] // PIECES
+    for piece in range(PIECES):
+        arrive(piece)
+        for at in range(size // 16):
+            summed[piece * (size // 16) + at] = total(pl.ds(piece * size + at * 16, 16)).astype(jnp.bfloat16)
+    local.append(copies.local(summed.at[me], att_out.at[me]))
+    for dc, dy in others:
+        to_core, to_y = there(dc, dy)
+        to = {"core": to_core, "y": to_y}
+        back.append(copies.start(summed.at[to_core * 4 + to_y], att_out.at[me], to))
+    for copy in back:
+        copy.wait_recv()
+    copies.finish()
+    for copy in local:
+        copy.wait()
+
+
+def call(kernel, number, ins, in_spaces, outs, out_spaces, scratch, sems, cost):
+    def spec(space):
+        return pl.BlockSpec(memory_space=space)
+
+    return pl.pallas_call(
+        kernel,
+        out_shape=[jax.ShapeDtypeStruct(shape, dtype) for shape, dtype in outs],
+        in_specs=[spec(space) for space in in_spaces],
+        out_specs=[spec(space) for space in out_spaces],
+        scratch_shapes=list(scratch)
+        + [pltpu.SemaphoreType.DMA((sems,)), pltpu.SemaphoreType.DMA((sems,))],
+        compiler_params=pltpu.CompilerParams(
+            collective_id=number, has_side_effects=True, vmem_limit_bytes=VMEM_LIMIT
+        ),
+        cost_estimate=pl.CostEstimate(flops=cost, bytes_accessed=64 * 2**20, transcendentals=0),
+        name=kernel.__name__,
+    )(*ins)
+
+
+def ring_scratch(width):
+    return [
+        pltpu.VMEM((4, 128, width), jnp.float32),
+        pltpu.VMEM((4, 128, width), jnp.bfloat16),
+        pltpu.VMEM((4, 128, width), jnp.bfloat16),
+        pltpu.VMEM((3, 128, width), jnp.bfloat16),
+        pltpu.VMEM((3, 128, width), jnp.bfloat16),
+    ]
 
 
 def split_columns(weight, pad):
@@ -184,28 +744,54 @@
         ),
         axis=2,
     )
-    pack = jnp.swapaxes(jnp.concatenate((pack_att, pack_mlp), axis=2), 0, 1)
-    pack = lax.all_to_all(pack, COLUMNS, split_axis=0, concat_axis=0, tiled=True)
-    pack = pack.reshape(8 * depth, -1)
-    att = lax.all_gather(pack[:, :ATT_W], CHIPS, axis=0, tiled=True)
-    mlp = lax.all_gather(pack[:, ATT_W:], CHIPS, axis=0, tiled=True)
+    hbm, vmem = pl.ANY, pltpu.VMEM
+    low_type, wide_type = jnp.bfloat16, jnp.float32
+    forth, back = lane_order(False), lane_order(True)
+    raw = reorder(hidden_in.reshape(toks, width), forth, False)
+    scale = row_scale(source_id, source_counts)
+    top = (cotangent.astype(jnp.float32) * scale[:, None, None]).reshape(toks, width)
+    top = reorder(top.astype(jnp.bfloat16), forth, False)
+    att, mlp, raw, top = call(
+        spread_kernel,
+        0,
+        (jnp.swapaxes(pack_att, 0, 1), jnp.swapaxes(pack_mlp, 0, 1), raw, top),
+        [hbm] * 4,
+        [
+            ((8, depth, ATT_W), low_type),
+            ((8, depth, 3 * PAD_FF), low_type),
+            ((toks, width), low_type),
+            ((toks, width), low_type),
+        ],
+        [hbm] * 4,
+        [],
+        18,
+        0,
+    )
+    mlp = lax.all_gather(mlp.reshape(8 * depth, 3 * PAD_FF), CHIPS, axis=0, tiled=True)
+    grad_low = whole_row(top)
+    raw_full, att = call(
+        first_kernel,
+        1,
+        (raw, att.reshape(8 * depth, ATT_W)),
+        [hbm] * 2,
+        [((8, toks, width), low_type), ((16, 8 * depth, ATT_W), low_type)],
+        [hbm] * 2,
+        [],
+        80,
+        0,
+    )
+    length = 8 * toks
+    raw_full = raw_full.reshape(length, width)
+    att = att.reshape(width, ATT_W)
     w_value, w_out = att[:, :256], att[:, 256:512]
     w_query, w_key = att[:, 512:544], att[:, 544:576]
-    norm1 = att[:, 576].astype(jnp.float32)
-    norm2 = att[:, 577].astype(jnp.float32)
+    gains = att[:, 576:578].astype(jnp.float32).T
+    norm1, norm2 = gains[:1], gains[1:]
     w_gate, w_up, w_down = mlp[:, :PAD_FF], mlp[:, PAD_FF : 2 * PAD_FF], mlp[:, 2 * PAD_FF :]
 
-    forth, back = lane_order(False), lane_order(True)
-    raw = swap(reorder(hidden_in.reshape(toks, width), forth, False))
-    scale = row_scale(source_id, source_counts)
-    top = (cotangent.astype(jnp.float32) * scale[:, None, None]).reshape(toks, width)
-    top_low = swap(reorder(top.astype(jnp.bfloat16), forth, False))
-    grad_top = top_low.astype(jnp.float32)
-
-    inputs = raw.astype(jnp.float32)
+    inputs = raw_full.astype(jnp.float32)
     inverse1 = lax.rsqrt(jnp.mean(inputs * inputs, axis=-1, keepdims=True) + norm_eps)
-    normed = whole_row((inputs * inverse1 * norm1).astype(jnp.bfloat16))
-    length = normed.shape[0]
+    normed = (inputs * inverse1 * norm1).astype(jnp.bfloat16)
     heads_here = w_query.shape[1] // FEAT
     query = dot(normed, w_query).reshape(length, heads_here, FEAT)
     keys = dot(normed, w_key).reshape(length, heads_here, FEAT)
@@ -214,25 +800,41 @@
     feat_k = taylor(keys).astype(jnp.bfloat16)
     scores, denom, mixed = attend(feat_q, feat_k, values)
     attended = mixed.astype(jnp.bfloat16).reshape(length, heads_here * HEAD_V)
-    middle = inputs + own_rows(((attended, w_out),))
-    inverse2 = lax.rsqrt(jnp.mean(middle * middle, axis=-1, keepdims=True) + norm_eps)
-    normed2 = whole_row((middle * inverse2 * norm2).astype(jnp.bfloat16))
-    grad_low = whole_row(top_low)
+    middle, normed2 = call(
+        middle_kernel,
+        2,
+        (attended, att, raw, norm2),
+        [vmem] * 4,
+        [((toks, width), wide_type), ((8, toks, width), low_type)],
+        [vmem, hbm],
+        ring_scratch(width) + [vmem((toks, width), low_type)],
+        36,
+        10**9,
+    )
+    normed2 = normed2.reshape(length, width)
     gate = dot(normed2, w_gate)
     upward = dot(normed2, w_up)
     sigma = jax.nn.sigmoid(gate)
     hidden = (gate * sigma * upward).astype(jnp.bfloat16)
-    grad_down = contract_rows(grad_low, hidden).astype(jnp.bfloat16)
     grad_hidden = dot(grad_low, w_down)
     gate_act = (grad_hidden * upward * sigma * (1.0 + gate * (1.0 - sigma))).astype(jnp.bfloat16)
     up_act = (grad_hidden * gate * sigma).astype(jnp.bfloat16)
-    grad_normed2 = own_rows(((gate_act, w_gate), (up_act, w_up)))
+    grad_middle, grad_norm2, middle_low = call(
+        middle_back_kernel,
+        3,
+        (gate_act, up_act, mlp, middle, top, norm2),
+        [vmem] * 6,
+        [((toks, width), wide_type), ((8, width), wide_type), ((8, toks, width), low_type)],
+        [vmem, vmem, hbm],
+        ring_scratch(width) + [vmem((toks, width), low_type)],
+        36,
+        6 * 10**9,
+    )
+    middle_low = middle_low.reshape(length, width)
     layer_out = (middle + own_rows(((hidden, w_down),))).astype(jnp.bfloat16)
+    grad_down = contract_rows(grad_low, hidden).astype(jnp.bfloat16)
     grad_gate = contract_rows(normed2, gate_act).astype(jnp.bfloat16)
     grad_up = contract_rows(normed2, up_act).astype(jnp.bfloat16)
-    grad_mid_norm, grad_norm2 = norm_back(grad_normed2, middle, inverse2, norm2)
-    grad_middle = grad_top + grad_mid_norm
-    middle_low = whole_row(grad_middle.astype(jnp.bfloat16))
     grads_mlp = lax.psum_scatter(
         jnp.concatenate((grad_gate, grad_up, grad_down), axis=1),
         CHIPS,
@@ -246,44 +848,70 @@
     )
     grad_values = grad_values.astype(jnp.bfloat16).reshape(length, heads_here * HEAD_V)
     grad_q, grad_k = feature_back(query, keys, grad_feat_q, grad_feat_k, length)
-    grad_query = contract_rows(normed, grad_q).astype(jnp.bfloat16)
-    grad_key = contract_rows(normed, grad_k).astype(jnp.bfloat16)
+    grad_qk = jnp.pad(jnp.concatenate((grad_q, grad_k), axis=1), ((0, 0), (0, 64)))
+    grad_in, grad_norm1 = call(
+        input_back_kernel,
+        4,
+        (grad_qk, grad_values, att, raw, grad_middle, norm1),
+        [vmem] * 6,
+        [((toks, width), low_type), ((8, width), wide_type)],
+        [vmem] * 2,
+        ring_scratch(width),
+        36,
+        10**9,
+    )
+    grad_qk = contract_rows(normed, grad_qk)
     grad_value = contract_rows(normed, grad_values).astype(jnp.bfloat16)
-    grad_normed = own_rows(((grad_q, w_query), (grad_k, w_key), (grad_values, w_value)))
-    grad_in_norm, grad_norm1 = norm_back(grad_normed, inputs, inverse1, norm1)
-    grad_in = (grad_middle + grad_in_norm).astype(jnp.bfloat16)
-    grad_pair = jnp.stack((grad_norm1, grad_norm2), axis=1).astype(jnp.bfloat16)
-    grads_att = lax.psum_scatter(
-        jnp.concatenate(
-            (grad_value, grad_out, grad_query, grad_key, jnp.pad(grad_pair, ((0, 0), (0, 62)))),
-            axis=1,
+    grad_pair = jnp.stack((jnp.sum(grad_norm1, axis=0), jnp.sum(grad_norm2, axis=0)), axis=1)
+    grads_att = jnp.concatenate(
+        (
+            grad_value,
+            grad_out,
+            grad_qk[:, :64].astype(jnp.bfloat16),
+            jnp.pad(grad_pair, ((0, 0), (0, 62))).astype(jnp.bfloat16),
         ),
-        CHIPS,
-        scatter_dimension=0,
-        tiled=True,
-    )
-    summed = jnp.concatenate((grads_att, grads_mlp), axis=1).reshape(8, depth, -1)
-    summed = lax.all_to_all(summed, COLUMNS, split_axis=0, concat_axis=0, tiled=True)
-    summed = jnp.swapaxes(summed, 0, 1).astype(jnp.float32)
-
-    def joined(start, size):
-        return summed[:, :, start : start + size].reshape(depth, 8 * size)
-
-    pair = jnp.sum(summed[:, :, 576:578], axis=1)
+        axis=1,
+    )
+    rows_here = 8 * depth
+    grads_att, grads_mlp = call(
+        last_kernel,
+        5,
+        (grads_att.reshape(16, rows_here, ATT_W), grads_mlp.reshape(8, depth, 3 * PAD_FF)),
+        [vmem, hbm],
+        [((8, depth, ATT_W), low_type), ((8, depth, 3 * PAD_FF), low_type)],
+        [hbm] * 2,
+        [
+            vmem((4, 3, rows_here, ATT_W), low_type),
+            vmem((4, 3, rows_here, ATT_W), low_type),
+            vmem((4, rows_here, ATT_W), wide_type),
+            vmem((3, rows_here, ATT_W), low_type),
+            vmem((3, rows_here, ATT_W), low_type),
+            vmem((8, depth, ATT_W), low_type),
+        ],
+        80,
+        0,
+    )
+    att_sums = jnp.swapaxes(grads_att, 0, 1).astype(jnp.float32)
+    mlp_sums = jnp.swapaxes(grads_mlp, 0, 1).astype(jnp.float32)
+
+    def joined(sums, start, size):
+        return sums[:, :, start : start + size].reshape(depth, 8 * size)
+
+    pair = jnp.sum(att_sums[:, :, 576:578], axis=1)
     layer_out = reorder(swap(layer_out), back, True).reshape(rows, toks, width)
     grad_in = reorder(swap(grad_in), back, True).astype(jnp.float32).reshape(rows, toks, width)
     return (
         layer_out,
         grad_in,
         pair[:, 0],
-        joined(512, 32),
-        joined(544, 32),
-        joined(0, 256),
-        joined(256, 256),
+        joined(att_sums, 512, 32),
+        joined(att_sums, 544, 32),
+        joined(att_sums, 0, 256),
+        joined(att_sums, 256, 256),
         pair[:, 1],
-        joined(ATT_W, ff_here),
-        joined(ATT_W + PAD_FF, ff_here),
-        joined(ATT_W + 2 * PAD_FF, ff_here),
+        joined(mlp_sums, 0, ff_here),
+        joined(mlp_sums, PAD_FF, ff_here),
+        joined(mlp_sums, 2 * PAD_FF, ff_here),
     )
 
 

time: 721 us -> 460 us (0.64)
  waiting for transfers between devices: 472 us -> 0.83 us
  Pallas kernels: 0 us -> 276 us
  starting transfers between devices: 32.4 us -> 8.12 us
  matrix products: 105 us -> 83.6 us
  blocking collectives: 17.6 us -> 0 us
    pallas_call x0 -> x6, Pallas kernels: none -> 276 us  [call(): pl.pallas_call(kernel, out_shape=[jax.ShapeDtypeStruct(shape, dtype) for...]
    all_gather x4 -> x1, waiting for transfers between devices: 116 us -> 0.01 us  [whole_row(): return lax.all_gather(piece, TOKENS, axis=0, tiled=True)]
    all_gather x2 -> x1, waiting for transfers between devices: 83.7 us -> 0.02 us  [body(): lax.all_gather(mlp.reshape(8 * depth, 3 * PAD_FF), CHIPS, axis=0, tiled=T...]
    reduce_scatter x4 -> x1, waiting for transfers between devices: 83.7 us -> 0.02 us  [own_rows(): lax.psum_scatter(total.astype(jnp.bfloat16), TOKENS, scatter_dimension=0,...]
    reduce_scatter x1, waiting for transfers between devices: 80.7 us -> 0.01 us  [body(): lax.psum_scatter(jnp.concatenate((grad_gate, grad_up, grad_down), axis=1)...]
    reduce_scatter x1 -> x0, waiting for transfers between devices: 77.5 us -> none  [body(): lax.psum_scatter(jnp.concatenate((grad_value, grad_out, grad_query, grad_...]
    dot_general x7 -> x1, matrix products: 30 us -> 6.84 us  [contract_cols(): lax.dot_general(left, right, (((1,), (1,)), ((), ())), preferred_element_...]
    ppermute x4 -> x2, waiting for transfers between devices: 21 us -> 0.04 us  [swap(): lax.ppermute(array, ('core', 'zhi'), [(0, 0), (1, 2), (2, 1), (3, 3)])]
  transfers between devices with their start and end apart: 17 -> 6, of which waited for: 14 -> 0; matrix products, arithmetic and copies ran while one was open for 12% -> 25% of each run, Pallas kernels for 0% -> 47%
where the time goes in v2:
time: 460 us; the launch traced here: 456 us
  Pallas kernels  276 us (60%)
  matrix products  83.6 us (18%)
  local copies, waits for them, and re-layouts  47.7 us (10%)
  other arithmetic  23.3 us (5%)
  between operations  16.3 us (4%)
  starting transfers between devices  8.12 us (2%)
    pallas_call x6, Pallas kernels, call(): pl.pallas_call(kernel, out_shape=[jax.ShapeDtypeStruct(shape, dtype) for...  276 us
    dot_general x11, matrix products, dot(): return jnp.dot(left, right, preferred_element_type=jnp.float32)  37.5 us
    unnamed x76, local copies, waits for them, and re-layouts  22.9 us
    dot_general x6, matrix products, contract_rows(): lax.dot_general(left, right, (((0,), (0,)), ((), ())), preferred_element_...  19.6 us
  transfers between devices with their start and end apart: 6, of which 0 were waited for; matrix products, arithmetic and copies ran while one was open for 25% of the time, Pallas kernels for 47%

profile of v2, /device:TPU:1, one launch (start us, length us, event | category | flops | bytes accessed | tf_op | source)
XLA Modules:
  0.0 456.2 jit_solution(1764220493739687130)
XLA Ops:
  20.9 21.2 %spread_kernel.1 = (bf16[8,16,640]{2,1,0:T(8,128)(2,1)S(1)}, bf16[8,16,2304]{2,1,0:T(8,128)(2,1)}, bf16[128,2048]{1,0:T(8,128)(2,1)S(1)}, bf16[128,2048]{1,0:T(8,128)(2,1)}) custom-call(bf16[8,16,640]{2,1,0:T(8,128)(2,1)S(1)} %bitcast.143, bf16[8,16,2304]{2,1,0:T(8,128)(2,1)} %fusion.46.mlp, bf16[128,2048]{1,0:T(8,128)(2,1)S(1)} %get-tuple-element.76.raw, ...), custom_call_target="tpu_custom_call" | custom-call | bytes 67108864 | tf_op jit(solution)/shard_map/spread_kernel/pallas_call | solution.py:677
  43.4 46.6 %first_kernel.1 = (bf16[8,128,2048]{2,1,0:T(8,128)(2,1)}, bf16[16,128,640]{2,1,0:T(8,128)(2,1)}) custom-call(bf16[128,2048]{1,0:T(8,128)(2,1)S(1)} %get-tuple-element.26.raw, bf16[128,640]{1,0:T(8,128)(2,1)S(1)} %bitcast.145), custom_call_target="tpu_custom_call" | custom-call | bytes 67108864 | tf_op jit(solution)/shard_map/first_kernel/pallas_call | solution.py:677
  91.3 1.6 fusion.72
  93.9 3.8 multiply_reduce_fusion
  98.8 1.3 multiply_convert_fusion.7
  103.4 3.4 convolution_convert_fusion.10
  106.8 3.6 select_reduce_fusion
  110.5 2.5 fusion.76
  113.1 69.6 %middle_kernel.1 = (f32[128,2048]{1,0:T(8,128)}, bf16[8,128,2048]{2,1,0:T(8,128)(2,1)}) custom-call(bf16[1024,256]{1,0:T(8,128)(2,1)S(1)} %copy.148.attended, bf16[2048,640]{1,0:T(8,128)(2,1)} %bitcast.151, bf16[128,2048]{1,0:T(8,128)(2,1)S(1)} %get-tuple-element.26.raw, f32[1,2048]{1,0:T(1,128)S(1)} %get-tuple-element.59.gain), custom_call_target="tpu_custom_call" | custom-call | flops 1000000000 | bytes 67108864 | tf_op jit(solution)/shard_map/middle_kernel/pallas_call | solution.py:677
  182.8 8.4 %fusion.20 = f32[1024,768]{1,0:T(8,128)} fusion(bf16[1024,2048]{1,0:T(8,128)(2,1)} %bitcast.192, bf16[2048,2304]{1,0:T(8,128)(2,1)} %all-gather.3.cloned.1.call-done.mlp), kind=kOutput, calls=%fused_computation.31 | convolution fusion | flops 3221225472 | bytes 10485760 | tf_op jit(solution)/shard_map/dot_general | solution.py:36
  191.2 7.0 %fusion.18 = f32[1024,768]{1,0:T(8,128)} fusion(bf16[1024,2048]{1,0:T(8,128)(2,1)S(1)} %bitcast.194, bf16[2048,2304]{1,0:T(8,128)(2,1)} %all-gather.3.cloned.1.call-done.mlp), kind=kOutput, calls=%fused_computation.29 | convolution fusion | flops 3221225472 | bytes 10485760 | tf_op jit(solution)/shard_map/dot_general | solution.py:36
  198.3 11.0 %multiply_convert_fusion.1 = (bf16[1024,768]{1,0:T(8,128)(2,1)}, bf16[1024,768]{1,0:T(8,128)(2,1)}, bf16[1024,768]{1,0:T(8,128)(2,1)S(1)}) fusion(f32[1024,768]{1,0:T(8,128)} %fusion.20, f32[1024,768]{1,0:T(8,128)} %fusion.18, bf16[1024,2048]{1,0:T(8,128)(2,1)} %all-gather.5.cloned.1.call-done, bf16[2048,2304]{1,0:T(8,128)(2,1)} %all-gather.3.cloned.1.call-done.mlp), kind=kOutput, calls=%fused_computation.33 | convolution fusion | flops 3233808384 | bytes 18350080 | tf_op jit(solution)/shard_map/dot_general | solution.py:36
  210.3 6.8 %convolution_convert_fusion = bf16[1024,2048]{1,0:T(8,128)(2,1)} fusion(bf16[1024,768]{1,0:T(8,128)(2,1)S(1)} %get-tuple-element.49, bf16[2048,2304]{1,0:T(8,128)(2,1)} %all-gather.3.cloned.1.call-done.mlp), kind=kOutput, calls=%fused_computation.25 | convolution fusion | flops 3223322624 | bytes 8912896 | tf_op jit(solution)/shard_map/dot_general | solution.py:46
  217.5 6.3 %convolution_convert_fusion.2 = bf16[2048,768]{0,1:T(8,128)(2,1)S(1)} fusion(bf16[1024,2048]{1,0:T(8,128)(2,1)} %bitcast.193, bf16[1024,768]{1,0:T(8,128)(2,1)} %get-tuple-element.47.up_act), kind=kOutput, calls=%fused_computation.27 | convolution fusion | flops 3222798336 | bytes 8912896 | tf_op jit(solution)/shard_map/dot_general | solution.py:40
  223.8 3.8 convolution_convert_fusion.3
  227.7 3.8 convolution_convert_fusion.1
  231.6 4.3 pad_maximum_fusion
  235.9 12.8 %copy.150 = bf16[2048,2304]{1,0:T(8,128)(2,1)} copy(bf16[2048,2304]{0,1:T(8,128)(2,1)} %pad_maximum_fusion) | data formatting | bytes 18874368
  250.0 1.4 copy.156
  251.5 64.6 %middle_back_kernel.1 = (f32[128,2048]{1,0:T(8,128)S(1)}, f32[8,2048]{1,0:T(8,128)S(1)}, bf16[8,128,2048]{2,1,0:T(8,128)(2,1)}) custom-call(bf16[1024,768]{1,0:T(8,128)(2,1)} %get-tuple-element.48.gate_act, bf16[1024,768]{1,0:T(8,128)(2,1)} %get-tuple-element.47.up_act, bf16[2048,2304]{1,0:T(8,128)(2,1)} %all-gather.3.cloned.1.call-done.mlp, ...), custom_call_target="tpu_custom_call" | custom-call | flops 6000000000 | bytes 67108864 | tf_op jit(solution)/shard_map/middle_back_kernel/pallas_call | solution.py:677
  316.1 3.8 multiply_reduce_fusion.5
  321.5 2.0 fusion.26
  326.5 6.0 %fusion.25 = f32[1024,2,273]{0,2,1:T(8,128)S(1)} fusion(f32[2,1024,1024]{1,2,0:T(8,128)} %copy-done.3, f32[2,1024]{1,0:T(2,128)S(1)} %bitcast_divide_fusion, pred[1024,1024]{0,1:T(8,128)(4,1)} %copy-done.11, bf16[1024,2,256]{0,2,1:T(8,128)(2,1)} %bitcast.165, bf16[1024,2,16]{0,2,1:T(8,128)(2,1)S(1)} %get-tuple-element.63, bf16[273]{0:T(512)(128)(2,1)S(1)} %pad.43.clone), kind=kOutput, calls=%fused_computation.53 | convolution fusion | flops 1152593920 | bytes 12796450 | tf_op jit(solution)/shard_map/hts,shf->thf/dot_general | solution.py:73
  334.0 4.2 fusion.30
  338.6 34.7 %input_back_kernel.1 = (bf16[128,2048]{1,0:T(8,128)(2,1)S(1)}, f32[8,2048]{1,0:T(8,128)S(1)}) custom-call(bf16[1024,128]{1,0:T(8,128)(2,1)S(1)} %fusion.57.grad_qk, bf16[1024,256]{1,0:T(8,128)(2,1)S(1)} %copy.149.grad_values, bf16[2048,640]{1,0:T(8,128)(2,1)} %bitcast.153, bf16[128,2048]{1,0:T(8,128)(2,1)S(1)} %get-tuple-element.26.raw, ...), custom_call_target="tpu_custom_call" | custom-call | flops 1000000000 | bytes 67108864 | tf_op jit(solution)/shard_map/input_back_kernel/pallas_call | solution.py:677
  373.3 3.7 collective-permute-start.1
  377.1 3.1 fusion.77
  384.3 2.3 add_convert_fusion
  386.6 3.5 collective-permute-start
  390.2 1.7 pad_maximum_fusion.1
  391.9 4.4 copy.131
  402.5 39.6 %last_kernel.1 = (bf16[8,16,640]{2,1,0:T(8,128)(2,1)S(1)}, bf16[8,16,2304]{2,1,0:T(8,128)(2,1)S(1)}) custom-call(bf16[16,128,640]{2,1,0:T(8,128)(2,1)} %bitcast.154, bf16[8,16,2304]{2,1,0:T(8,128)(2,1)S(1)} %bitcast.144), custom_call_target="tpu_custom_call" | custom-call | bytes 67108864 | tf_op jit(solution)/shard_map/last_kernel/pallas_call | solution.py:677
  (168 shorter events, 46.9 us)
Async XLA Ops:
  7.2 10.7 %copy-start.14 = (bf16[256,256]{1,0:T(8,128)(2,1)S(1)}, bf16[256,256]{1,0:T(8,128)(2,1)}, u32[]{:S(2)}) copy-start(bf16[256,256]{1,0:T(8,128)(2,1)} %constant.37.clone) | copy-start | bytes 393220
  7.2 10.5 %copy-start.15 = (bf16[1,128,2048]{2,1,0:T(8,128)(2,1)S(1)}, bf16[1,128,2048]{2,1,0:T(8,128)(2,1)}, u32[]{:S(2)}) copy-start(bf16[1,128,2048]{2,1,0:T(8,128)(2,1)} %param.15) | copy-start | bytes 1572868
  7.2 175.6 %all-gather.3.cloned.1.call-start = ((), (), s32[]{:S(2)}) async-start(), calls=%async_computation.2 | async-start | bytes 10027008 | tf_op jit(solution)/shard_map/all_gather | solution.py:770
  16.2 2.6 copy-start.21
  16.2 2.6 copy-start.22
  42.1 156.2 %all-gather.5.cloned.1.call-start = ((), (), s32[]{:S(2)}) async-start(), calls=%async_computation.4 | async-start | bytes 4718592 | tf_op jit(solution)/shard_map/all_gather | solution.py:123
  42.9 341.5 %reduce-scatter.5.cloned.1.call-start = ((), (), s32[]{:S(2)}) async-start(), calls=%async_computation.3 | async-start | bytes 4718592 | tf_op jit(solution)/shard_map/reduce_scatter | solution.py:131
  93.6 4.2 copy-start.2
  93.9 16.6 %copy-start.11 = (pred[1024,1024]{0,1:T(8,128)(4,1)}, pred[1024,1024]{0,1:T(8,128)(4,1)S(1)}, u32[]{:S(2)}) copy-start(pred[1024,1024]{0,1:T(8,128)(4,1)S(1)} %iota_compare_fusion) | copy-start | bytes 3145732
  100.4 6.4 %copy-start.7 = (bf16[1024,2,16,16]{0,3,2,1:T(8,128)(2,1)}, bf16[1024,2,16,16]{0,3,2,1:T(8,128)(2,1)S(1)}, u32[]{:S(2)}) copy-start(bf16[1024,2,16,16]{0,3,2,1:T(8,128)(2,1)S(1)} %multiply_convert_fusion.4) | copy-start | bytes 3145732
  102.1 4.7 %copy-start.27 = (bf16[1024,2,16]{0,2,1:T(8,128)(2,1)}, bf16[1024,2,16]{0,2,1:T(8,128)(2,1)S(1)}, u32[]{:S(2)}) copy-start(bf16[1024,2,16]{0,2,1:T(8,128)(2,1)S(1)} %get-tuple-element.65) | copy-start | bytes 196612
  102.4 4.4 copy-start.8
  103.4 3.4 copy-start.6
  110.4 2.5 copy-start.30
  112.9 78.3 %copy-start.16 = (bf16[1024,2,128]{0,2,1:T(8,128)(2,1)}, bf16[1024,2,128]{0,2,1:T(8,128)(2,1)S(1)}, u32[]{:S(2)}) copy-start(bf16[1024,2,128]{0,2,1:T(8,128)(2,1)S(1)} %get-tuple-element.69) | copy-start | bytes 1572868
  182.8 8.4 %copy-start.25 = (bf16[8,128,2048]{2,1,0:T(8,128)(2,1)S(1)}, bf16[8,128,2048]{2,1,0:T(8,128)(2,1)}, u32[]{:S(2)}) copy-start(bf16[8,128,2048]{2,1,0:T(8,128)(2,1)} %get-tuple-element.31) | copy-start | bytes 12582916
  217.2 184.2 %reduce-scatter.7.cloned.1.call-start = ((), (), s32[]{:S(2)}) async-start(), calls=%async_computation.5 | async-start | bytes 10027008 | tf_op jit(solution)/shard_map/reduce_scatter | solution.py:838
  217.5 6.3 %copy-start.26 = (bf16[8,128,2048]{2,1,0:T(8,128)(2,1)S(1)}, bf16[8,128,2048]{2,1,0:T(8,128)(2,1)}, u32[]{:S(2)}) copy-start(bf16[8,128,2048]{2,1,0:T(8,128)(2,1)} %get-tuple-element.31) | copy-start | bytes 12582916
  217.5 6.3 %copy-start.31 = (bf16[1024,768]{1,0:T(8,128)(2,1)S(1)}, bf16[1024,768]{1,0:T(8,128)(2,1)}, u32[]{:S(2)}) copy-start(bf16[1024,768]{1,0:T(8,128)(2,1)} %get-tuple-element.48.gate_act) | copy-start | bytes 4718596
  223.8 3.9 copy-start.23
  223.8 3.9 copy-start.33
  251.5 64.6 %copy-start.13 = (bf16[2048,256]{0,1:T(8,128)(2,1)S(1)}, bf16[2048,256]{0,1:T(8,128)(2,1)}, u32[]{:S(2)}) copy-start(bf16[2048,256]{0,1:T(8,128)(2,1)} %copy.156) | copy-start | bytes 3145732
  251.5 64.6 %copy-start.29 = (f32[1024,2,128]{0,2,1:T(8,128)S(1)}, f32[1024,2,128]{0,2,1:T(8,128)}, u32[]{:S(2)}) copy-start(f32[1024,2,128]{0,2,1:T(8,128)} %get-tuple-element.70) | copy-start | bytes 3145732
  316.1 3.9 copy-start
  321.5 3.3 copy-start.3
  338.2 35.1 %copy-start.18 = (bf16[2,128,1024]{2,1,0:T(8,128)(2,1)}, bf16[2,128,1024]{2,1,0:T(8,128)(2,1)S(1)}, u32[]{:S(2)}) copy-start(bf16[2,128,1024]{2,1,0:T(8,128)(2,1)S(1)} %fusion.30) | copy-start | bytes 1572868
  373.3 22.9 %collective-permute-start.1 = (bf16[128,2048]{1,0:T(8,128)(2,1)S(1)}, bf16[128,2048]{1,0:T(8,128)(2,1)}, u32[]{:S(2)}, u32[]{:S(2)}) collective-permute-start(bf16[128,2048]{1,0:T(8,128)(2,1)S(1)} %get-tuple-element.36), channel_id=1, source_target_pairs={{0,0},{1,8},{8,1},{9,9},{2,2},{3,10},{10,3},{11,11},{4,4},{5,12},{... | collective-permute-start | bytes 1572872 | tf_op jit(solution)/shard_map/ppermute | solution.py:119
  377.1 3.2 copy-start.17
  377.1 3.6 copy-start.24
  383.0 7.1 %slice-start = ((bf16[2048,128]{0,1:T(8,128)(2,1)}), bf16[2048,64]{0,1:T(8,128)(2,1)S(1)}, s32[]{:S(2)}) async-start(bf16[2048,128]{0,1:T(8,128)(2,1)} %copy-done.10), calls=%async_computation.6 | async-start | bytes 524288 | tf_op jit(solution)/shard_map/slice | solution.py:870
  386.6 12.3 %collective-permute-start = (bf16[128,2048]{1,0:T(8,128)(2,1)}, bf16[128,2048]{1,0:T(8,128)(2,1)}, u32[]{:S(2)}, u32[]{:S(2)}) collective-permute-start(bf16[128,2048]{1,0:T(8,128)(2,1)} %add_convert_fusion), channel_id=1, source_target_pairs={{0,0},{1,8},{8,1},{9,9},{2,2},{3,10},{10,3},{11,11},{4,4},{5,12},{... | collective-permute-start | bytes 1572872 | tf_op jit(solution)/shard_map/ppermute | solution.py:119
  391.8 5.6 %copy-start.20 = (bf16[256,256]{1,0:T(8,128)(2,1)S(1)}, bf16[256,256]{1,0:T(8,128)(2,1)}, u32[]{:S(2)}) copy-start(bf16[256,256]{1,0:T(8,128)(2,1)} %constant.38.clone) | copy-start | bytes 393220
  (9 other events, 14.8 us)
Sparse Core Ops, SparseCore 0:
  42.2 80.6 all-gather.2
  124.6 44.4 all-gather.4
  217.3 31.9 reduce-scatter.4
  252.6 88.3 reduce-scatter.6

commit v3 on v1

v3 whole, which is shorter than its diff:
```python
import jax
import jax.numpy as jnp
import numpy as np
from jax import lax
from jax.experimental import pallas as pl
from jax.experimental.pallas import tpu as pltpu
from jax.sharding import Mesh, PartitionSpec as P

FEAT = 16
HEAD_V = 128
PAD_FF = 768
ATT_W = 640
QK_AT = slice(512, 640)
OUT_AT = slice(256, 512)
VALUE_AT = slice(0, 256)

norm_eps = 1e-05
AXES = ("zlo", "x", "core", "y", "zhi")
DP = ("zlo", "x", "core")
SEQ = ("y", "zhi")
CHIPS = ("zhi", "zlo", "x")

MESH = pl.DeviceIdType.MESH
VMEM_LIMIT = 61 * 2**20
PIECES = 4
TILE = 256
STEP = 16
BF16, F32 = jnp.bfloat16, jnp.float32


def row_scale(source_id, source_counts):
    picked = jnp.sum(
        jnp.where(
            source_id[:, None] == jnp.arange(source_counts.shape[0], dtype=jnp.int32)[None, :],
            source_counts[None, :],
            0,
        ),
        axis=1,
    )
    return 4.0 / jnp.sqrt(picked.astype(F32))


def lane_order(back):
    at = np.arange(256)
    to = (at // 16 % 2) * 128 + (at // 32) * 16 + at % 16
    hot = np.zeros((256, 256), np.float32)
    hot[at, to] = 1.0
    return jnp.asarray(hot.T if back else hot, BF16)


def place():
    z = lax.axis_index("zhi") * 2 + lax.axis_index("zlo")
    return lax.axis_index("x"), lax.axis_index("y"), z, lax.axis_index("core")


def around(index):
    return lax.rem(index + 8, 4)


def at_y(y):
    return {"y": around(y)}


def at_core(core):
    return {"core": core}


def at_xz(x, z):
    x, z = around(x), around(z)
    return {"x": x, "zhi": z // 2, "zlo": lax.rem(z, 2)}


def ring_peers(y, core):
    return [at_y(y + 1), at_y(y - 1), at_core(1 - core)]


def plane_peers(x, z):
    return [at_xz(x + 1, z), at_xz(x - 1, z), at_xz(x, z + 1), at_xz(x, z - 1)]


def group_peers(y, core):
    return [
        (lax.rem(core + dc, 2), lax.rem(y + dy, 4))
        for dc in (0, 1)
        for dy in range(4)
        if (dc, dy) != (0, 0)
    ]


def greet(devices, partner=None, swaps=None):
    barrier = pltpu.get_barrier_semaphore()
    for device in devices:
        pl.semaphore_signal(barrier, inc=1, device_id=device, device_id_type=MESH)
    count = len(devices)
    if partner is not None:

        @pl.when(swaps)
        def _():
            pl.semaphore_signal(barrier, inc=1, device_id=partner, device_id_type=MESH)

        count = count + jnp.where(swaps, 1, 0)
    pl.semaphore_wait(barrier, count)


class Copies:
    def __init__(self, send, recv):
        self.send, self.recv, self.used, self.open = send, recv, 0, []

    def start(self, src, dst, device):
        copy = pltpu.make_async_remote_copy(
            src_ref=src,
            dst_ref=dst,
            send_sem=self.send.at[self.used],
            recv_sem=self.recv.at[self.used],
            device_id=device,
            device_id_type=MESH,
        )
        copy.start()
        self.used += 1
        self.open.append(copy)
        return copy

    def local(self, src, dst):
        copy = pltpu.make_async_copy(src, dst, self.send.at[self.used])
        copy.start()
        self.used += 1
        return copy

    def swap(self, src, dst, partner, swaps):
        at = self.used
        self.used += 1

        def over():
            return pltpu.make_async_remote_copy(
                src_ref=src,
                dst_ref=dst,
                send_sem=self.send.at[at],
                recv_sem=self.recv.at[at],
                device_id=partner,
                device_id_type=MESH,
            )

        def stay():
            return pltpu.make_async_copy(src, dst, self.send.at[at])

        @pl.when(swaps)
        def _():
            over().start()

        @pl.when(jnp.logical_not(swaps))
        def _():
            stay().start()

        def wait():
            @pl.when(swaps)
            def _():
                over().wait()

            @pl.when(jnp.logical_not(swaps))
            def _():
                stay().wait()

        return wait

    def finish(self):
        for copy in self.open:
            copy.wait_send()


def way(piece):
    return 1 if piece % 2 == 0 else -1


def slab(ref, block, rows, piece=None):
    if piece is None:
        return ref.at[pl.ds(pl.multiple_of(block * rows, 128), rows)]
    size = rows // PIECES
    return ref.at[pl.ds(pl.multiple_of(block * rows + piece * size, 32), size)]


def row_steps(start, size, act, step=STEP):
    @pl.loop(0, size // step)
    def _(at):
        act(pl.ds(pl.multiple_of(start + at * step, step), step))


class GatherRing:
    def __init__(self, copies, to, mine, full, block_of, me, rows):
        self.copies, self.to, self.full, self.block_of = copies, to, full, block_of
        self.me, self.rows, self.sent, self.onward = me, rows, {}, {}
        size = rows // PIECES
        for piece in range(PIECES):
            for step in (way(piece), -way(piece)):
                self.sent[step, piece] = copies.start(
                    mine.at[pl.ds(piece * size, size)],
                    slab(full, block_of(me), rows, piece),
                    to(me + step),
                )

    def forward(self):
        for piece in range(PIECES):
            step = way(piece)
            self.sent[step, piece].wait_recv()
            here = slab(self.full, self.block_of(self.me - step), self.rows, piece)
            self.onward[piece] = self.copies.start(here, here, self.to(self.me + step))

    def near(self):
        for piece in range(PIECES):
            self.sent[-way(piece), piece].wait_recv()

    def far(self):
        for piece in range(PIECES):
            self.onward[piece].wait_recv()


class GatherTokens:
    def __init__(self, copies, mine, full, y, core):
        self.copies, self.full, self.y, self.core = copies, full, y, core
        self.rows = mine.shape[0]
        self.shared = {}
        self.own = copies.local(mine, slab(full, self.block_of(y), self.rows))
        self.shared[0] = copies.start(mine, slab(full, self.block_of(y), self.rows), at_core(1 - core))
        self.ring = GatherRing(copies, at_y, mine, full, self.block_of, y, self.rows)

    def block_of(self, index):
        return around(index) * 2 + self.core

    def share(self, k):
        here = slab(self.full, self.block_of(self.y + k), self.rows)
        self.shared[k] = self.copies.start(here, here, at_core(1 - self.core))

    def forward(self):
        self.ring.forward()

    def near(self):
        self.ring.near()
        self.share(1)
        self.share(-1)

    def far(self):
        self.ring.far()
        self.share(2)

    def finish(self):
        self.own.wait()
        for copy in self.shared.values():
            copy.wait_recv()


class GatherPlane:
    def __init__(self, copies, mine, full, x, z, core):
        self.copies, self.full = copies, full
        rows = mine.shape[0]

        def block(a, b):
            a, b = around(a), around(b)
            return jnp.where(core == 0, 4 * b + a, 4 * a + b)

        first, second = jnp.where(core == 0, x, z), jnp.where(core == 0, z, x)

        def to_first(index):
            return at_xz(jnp.where(core == 0, index, x), jnp.where(core == 0, z, index))

        def to_second(index):
            return at_xz(jnp.where(core == 0, x, index), jnp.where(core == 0, index, z))

        def onto(k, source=None):
            a = first + k
            if source is None:
                source = slab(full, block(a, second), rows)
            return GatherRing(copies, to_second, source, full, lambda b: block(a, b), second, rows)

        self.onto = onto
        self.own = copies.local(mine, slab(full, block(first, second), rows))
        self.ring = GatherRing(
            copies, to_first, mine, full, lambda a: block(a, second), first, rows
        )
        self.rings = {0: onto(0, mine)}

    def stages(self):
        def one():
            self.ring.forward()

        def two():
            self.ring.near()
            self.rings[1] = self.onto(1)
            self.rings[-1] = self.onto(-1)

        def three():
            self.rings[0].forward()

        def four():
            self.ring.far()
            self.rings[2] = self.onto(2)

        def five():
            self.rings[1].forward()
            self.rings[-1].forward()

        def six():
            self.rings[2].forward()
            self.rings[0].near()
            self.rings[0].far()

        def seven():
            for k in (1, -1, 2):
                self.rings[k].near()
                self.rings[k].far()
            self.own.wait()

        return [one, two, three, four, five, six, seven]


class ReduceRing:
    def __init__(self, copies, to, me, read, out, got, rows, source=None):
        self.copies, self.to, self.me, self.read = copies, to, me, read
        self.out, self.got, self.rows, self.source, self.sent = out, got, rows, source, {}
        self.size = rows // PIECES

    def span(self, piece):
        return pl.ds(piece * self.size, self.size)

    def push(self, slot, k, piece, device):
        span = self.span(piece)
        if self.source is not None:
            ref = self.source(k, span)
        else:

            def fill(rows):
                self.out[slot, rows] = self.read(k, rows).astype(BF16)

            row_steps(piece * self.size, self.size, fill)
            ref = self.out.at[slot, span]
        self.sent[slot, piece] = self.copies.start(ref, self.got.at[slot, span], device)

    def far(self, pieces=range(PIECES)):
        for piece in pieces:
            self.push(0, 2, piece, self.to(self.me + way(piece)))

    def direct(self, k):
        for piece in range(PIECES):
            if way(piece) == -k:
                self.push(1, k, piece, self.to(self.me + k))

    def onward(self, k):
        slot = 2 if self.source is None else 0
        for piece in range(PIECES):
            if way(piece) == k:
                self.sent[0, piece].wait_recv()

                def fill(rows):
                    self.out[slot, rows] = (
                        self.read(k, rows) + self.got[0, rows].astype(F32)
                    ).astype(BF16)

                row_steps(piece * self.size, self.size, fill)
                span = self.span(piece)
                self.sent[2, piece] = self.copies.start(
                    self.out.at[slot, span], self.got.at[2, span], self.to(self.me + k)
                )

    def arrive(self, piece):
        self.sent[1, piece].wait_recv()
        self.sent[2, piece].wait_recv()

    def total(self, rows):
        return self.read(0, rows) + self.got[1, rows].astype(F32) + self.got[2, rows].astype(F32)


class ReduceTokens:
    def __init__(self, copies, make, y, core, own, sib, got_sib, out, got):
        self.copies, self.make, self.y, self.core = copies, make, y, core
        self.own, self.sib, self.got_sib, self.shared = own, sib, got_sib, {}
        self.ring = ReduceRing(copies, at_y, y, self.read, out, got, own.shape[1])

    def read(self, k, rows):
        return self.own[k % 4, rows] + self.got_sib[k % 4, rows].astype(F32)

    def part(self, k):
        self.make(k, self.own.at[k % 4], self.sib.at[k % 4])
        self.shared[k] = self.copies.start(
            self.sib.at[k % 4], self.got_sib.at[k % 4], at_core(1 - self.core)
        )

    def run(self):
        self.part(2)
        self.part(1)
        self.shared[2].wait_recv()
        self.ring.far()
        self.part(-1)
        self.shared[1].wait_recv()
        self.ring.direct(1)
        self.part(0)
        self.shared[-1].wait_recv()
        self.ring.direct(-1)
        self.ring.onward(1)
        self.ring.onward(-1)
        self.shared[0].wait_recv()

    def each(self, act):
        for piece in range(PIECES):
            self.ring.arrive(piece)

            def take(rows):
                act(rows, self.ring.total(rows))

            row_steps(piece * self.ring.size, self.ring.size, take)


class ReducePlane:
    def __init__(self, copies, parts, x, z, core, out1, got1, mid, out2, got2):
        rows = mid.shape[1]

        def block(a, b):
            a, b = around(a), around(b)
            return jnp.where(core == 0, 4 * b + a, 4 * a + b)

        last, first = jnp.where(core == 0, x, z), jnp.where(core == 0, z, x)

        def to_last(index):
            return at_xz(jnp.where(core == 0, index, x), jnp.where(core == 0, z, index))

        def to_first(index):
            return at_xz(jnp.where(core == 0, x, index), jnp.where(core == 0, index, z))

        def ring(k):
            def place_of(step, span):
                start = block(last + k, first + step) * rows + span.start
                return pl.ds(pl.multiple_of(start, STEP), span.size)

            def read(step, span):
                return parts[place_of(step, span)].astype(F32)

            def source(step, span):
                return parts.at[place_of(step, span)]

            return ReduceRing(copies, to_first, first, read, out1.at[k % 4], got1.at[k % 4], rows, source)

        self.mid = mid
        self.rings = {k: ring(k) for k in (2, 1, -1, 0)}

        def read2(step, span):
            return mid[step % 4, span].astype(F32)

        def source2(step, span):
            return mid.at[step % 4, span]

        self.ring = ReduceRing(copies, to_last, last, read2, out2, got2, rows, source2)

    def start(self):
        for ring in self.rings.values():
            ring.far()
            ring.direct(1)
            ring.direct(-1)

    def onward(self, k):
        self.rings[k].onward(1)
        self.rings[k].onward(-1)

    def middle(self, k):
        ring = self.rings[k]
        for piece in range(PIECES):
            ring.arrive(piece)

            def fill(rows):
                self.mid[k % 4, rows] = ring.total(rows).astype(BF16)

            row_steps(piece * ring.size, ring.size, fill)

    def stages(self):
        def ends(k, then):
            def act():
                self.middle(k)
                then()

            return act

        return (
            [self.start]
            + [lambda k=k: self.onward(k) for k in (2, 1, -1, 0)]
            + [
                ends(2, self.ring.far),
                ends(1, lambda: self.ring.direct(1)),
                ends(-1, lambda: self.ring.direct(-1)),
                ends(0, lambda: None),
                lambda: (self.ring.onward(1), self.ring.onward(-1)),
            ]
        )

    def each(self, act):
        for piece in range(PIECES):
            self.ring.arrive(piece)

            def take(rows):
                act(rows, self.ring.total(rows))

            row_steps(piece * self.ring.size, self.ring.size, take)


def nt(left, right):
    return lax.dot_general(left, right, (((1,), (1,)), ((), ())), preferred_element_type=F32)


def tn(left, right):
    return lax.dot_general(left, right, (((0,), (0,)), ((), ())), preferred_element_type=F32)


def nn(left, right):
    return jnp.dot(left, right, preferred_element_type=F32)


def chip_rows(block):
    return pl.ds(pl.multiple_of(block * 256, 256), 256)


def part_maker(pairs, y, core):
    def make(k, mine, theirs):
        rows = chip_rows(around(y + k))

        @pl.loop(0, mine.shape[-1] // TILE)
        def _(tile):
            columns = pl.ds(pl.multiple_of(tile * TILE, TILE), TILE)
            total = None
            for left, right, lanes in pairs:
                term = nt(left[rows, :], right[columns, lanes])
                total = term if total is None else total + term
            low, high = total[:128], total[128:]
            mine[:, columns] = jnp.where(core == 0, low, high)
            theirs[:, columns] = jnp.where(core == 0, high, low).astype(BF16)

    return make


def inverse_of(value):
    return lax.rsqrt(jnp.mean(value * value, axis=-1, keepdims=True) + norm_eps)


def norm_back_rows(grad, value, gain):
    inverse = inverse_of(value)
    unit = value * inverse
    scaled = grad * gain
    moved = inverse * (scaled - unit * jnp.mean(scaled * unit, axis=-1, keepdims=True))
    return moved, grad * unit


def reorder_into(target, source, hot):
    runs = source.shape[1] // 256
    for run in range(runs):
        moved = nn(source[:, run * 256 : (run + 1) * 256], hot[...]).astype(BF16)
        target[:, run * 128 : (run + 1) * 128] = moved[:, :128]
        target[:, (runs + run) * 128 : (runs + run + 1) * 128] = moved[:, 128:]


def spread_kernel(
    hidden,
    cotangent,
    scale,
    hot,
    query,
    key,
    value,
    out,
    gate,
    up,
    down,
    gains,
    att_out,
    mlp_out,
    raw_out,
    top_out,
    att,
    mlp,
    raw,
    top,
    send,
    recv,
):
    unused_x, y, z, core = place()
    zhi = z // 2
    partner = {"core": 1 - core, "zhi": 1 - zhi}
    swaps = core != zhi
    peers = group_peers(y, core)
    greet([{"core": c, "y": d} for c, d in peers], partner, swaps)
    copies = Copies(send, recv)
    me = core * 4 + y
    depth, here = gate.shape[0], gate.shape[1] // 8
    gap = jnp.zeros((depth, PAD_FF - here), BF16)
    for block in range(8):
        for at, weight in enumerate((gate, up, down)):
            cut = weight[:, block * here : (block + 1) * here]
            mlp[block, :, at * PAD_FF : (at + 1) * PAD_FF] = jnp.concatenate((cut, gap), axis=1)
    local = [copies.local(mlp.at[me], mlp_out.at[me])]
    got = []
    for c, d in peers:
        got.append(copies.start(mlp.at[c * 4 + d], mlp_out.at[me], {"core": c, "y": d}))
    reorder_into(raw, hidden, hot)
    waits = [copies.swap(raw, raw_out, partner, swaps)]
    gap = jnp.zeros((depth, 62), BF16)
    for block in range(8):
        att[block, :, VALUE_AT] = value[:, block * 256 : (block + 1) * 256]
        att[block, :, OUT_AT] = out[:, block * 256 : (block + 1) * 256]
        att[block, :, QK_AT] = jnp.concatenate(
            (
                query[:, block * 32 : (block + 1) * 32],
                key[:, block * 32 : (block + 1) * 32],
                gains[...],
                gap,
            ),
            axis=1,
        )
    local.append(copies.local(att.at[me], att_out.at[me]))
    for c, d in peers:
        got.append(copies.start(att.at[c * 4 + d], att_out.at[me], {"core": c, "y": d}))

    def weigh(rows):
        top[rows] = (cotangent[rows].astype(F32) * scale[...]).astype(BF16)

    row_steps(0, top.shape[0], weigh)
    reorder_into(top, top[...], hot)
    waits.append(copies.swap(top, top_out, partner, swaps))
    for copy in got:
        copy.wait_recv()
    copies.finish()
    for copy in local:
        copy.wait()
    for wait in waits:
        wait()


def gain_rows(att):
    row = lax.broadcasted_iota(jnp.int32, (8, 128), 0)
    lane = lax.broadcasted_iota(jnp.int32, (8, 128), 1)
    pick = jnp.where((lane == row + 64) & (row < 2), 1.0, 0.0).astype(BF16)
    return nt(pick, att[:, QK_AT])


def head_lanes(head):
    lane = lax.broadcasted_iota(jnp.int32, (1, 128), 1)
    return (lane >= head * FEAT) & (lane < (head + 1) * FEAT)


def scores_of(q, k, block, extent):
    x = nt(q, k) * 0.25
    row = lax.broadcasted_iota(jnp.int32, (256, extent), 0) + block * 256
    keep = row >= lax.broadcasted_iota(jnp.int32, (256, extent), 1)
    return x, jnp.where(keep, 1.0 + x + 0.5 * (x * x), 0.0), keep


def forward_kernel(
    raw,
    att,
    top,
    att_out,
    normed_out,
    low_out,
    qs,
    ks,
    values,
    attended,
    shares,
    gains,
    middle,
    normed2,
    raw_all,
    att_all,
    normed,
    own,
    sib,
    got_sib,
    out,
    got,
    low,
    send,
    recv,
):
    x, y, z, core = place()
    greet(ring_peers(y, core) + plane_peers(x, z))
    copies = Copies(send, recv)
    tokens = GatherTokens(copies, raw, raw_all, y, core)
    plane = GatherPlane(copies, att, att_all, x, z, core)
    one, two, three, four, five, six, seven = plane.stages()
    one()
    two()
    tokens.forward()
    three()
    four()
    tokens.near()
    five()
    six()
    tokens.far()
    seven()
    tokens.finish()
    tops = GatherTokens(copies, top, low_out, y, core)
    kept = [copies.local(att_all, att_out)]
    gains[...] = gain_rows(att_all)

    @pl.loop(0, 4)
    def _(chip):
        def norm(rows):
            value = raw_all[rows].astype(F32)
            normed[rows] = (value * inverse_of(value) * gains[0:1]).astype(BF16)

        row_steps(chip * 256, 256, norm)
        rows = chip_rows(chip)
        block = normed[rows]
        values[rows] = nn(block, att_all[:, VALUE_AT]).astype(BF16)
        both = nn(block, att_all[:, QK_AT])
        lane = lax.broadcasted_iota(jnp.int32, (1, 128), 1)
        qs[rows] = jnp.where(lane < 32, both, 0.0).astype(BF16)
        ks[rows] = jnp.where(lane < 32, pltpu.roll(both, 96, 1), 0.0).astype(BF16)

    kept.append(copies.local(normed, normed_out))
    for head in range(2):
        lanes = slice(head * HEAD_V, (head + 1) * HEAD_V)
        for block in range(4):
            rows, extent = slice(block * 256, (block + 1) * 256), (block + 1) * 256
            q = jnp.where(head_lanes(head), qs[rows], 0)
            unused, scores, unused_keep = scores_of(q, ks[0:extent], block, extent)
            share = 1.0 / jnp.sum(scores, axis=-1, keepdims=True)
            numer = nn(scores.astype(BF16), values[0:extent, lanes])
            attended[rows, lanes] = (numer * share).astype(BF16)
            shares[rows, lanes] = jnp.broadcast_to(share, (256, HEAD_V))
    sums = ReduceTokens(
        copies, part_maker([(attended, att_all, OUT_AT)], y, core), y, core, own, sib, got_sib, out, got
    )
    sums.run()
    tops.forward()

    def norm2(rows, total):
        value = raw[rows].astype(F32) + total
        middle[rows] = value
        low[rows] = (value * inverse_of(value) * gains[1:2]).astype(BF16)

    sums.each(norm2)
    back = GatherTokens(copies, low, normed2, y, core)
    tops.near()
    tops.far()
    back.forward()
    back.near()
    back.far()
    tops.finish()
    back.finish()
    for copy in kept:
        copy.wait()
    copies.finish()


def mlp_kernel(
    normed2_in,
    low_in,
    weights_in,
    middle,
    top,
    gains,
    grad_middle,
    grad_gain,
    middle_low,
    grads,
    layer_out,
    normed2,
    grad_low,
    weights,
    hidden,
    gate_act,
    up_act,
    stage,
    own,
    sib,
    got_sib,
    out,
    got,
    sib2,
    got_sib2,
    out2,
    got2,
    low,
    layer,
    send,
    recv,
):
    unused_x, y, z, core = place()
    zhi = z // 2
    partner = {"core": 1 - core, "zhi": 1 - zhi}
    swaps = core != zhi
    copies = Copies(send, recv)
    loads = [copies.local(weights_in, weights)]
    rows_in = {}
    for k in (2, 1, -1, 0):
        rows = chip_rows(around(y + k))
        rows_in[k] = [
            copies.local(normed2_in.at[rows], normed2.at[rows]),
            copies.local(low_in.at[rows], grad_low.at[rows]),
        ]
    greet(ring_peers(y, core), partner, swaps)
    for copy in loads:
        copy.wait()

    def act_block(k):
        for copy in rows_in[k]:
            copy.wait()
        rows = chip_rows(around(y + k))

        @pl.loop(0, PAD_FF // TILE)
        def _(tile):
            def lanes(at):
                return pl.ds(pl.multiple_of(at * PAD_FF + tile * TILE, TILE), TILE)

            block = normed2[rows]
            gate = nn(block, weights[:, lanes(0)])
            upward = nn(block, weights[:, lanes(1)])
            grad_hidden = nn(grad_low[rows], weights[:, lanes(2)])
            sigma = jax.nn.sigmoid(gate)
            silu = gate * sigma
            hidden[rows, lanes(0)] = (silu * upward).astype(BF16)
            slope = sigma + silu * (1.0 - sigma)
            gate_act[rows, lanes(0)] = (grad_hidden * upward * slope).astype(BF16)
            up_act[rows, lanes(0)] = (grad_hidden * silu).astype(BF16)

    base = part_maker(
        [(gate_act, weights, slice(0, PAD_FF)), (up_act, weights, slice(PAD_FF, 2 * PAD_FF))], y, core
    )

    def make(k, mine, theirs):
        act_block(k)
        base(k, mine, theirs)

    stored = []

    def grad_block(at, left, right):
        if stored:
            stored[-1].wait()

        @pl.loop(0, left.shape[1] // TILE)
        def _(tile):
            columns = pl.ds(pl.multiple_of(tile * TILE, TILE), TILE)
            stage[columns] = tn(left[:, columns], right[...]).astype(BF16)

        stored.append(copies.local(stage, grads.at[:, pl.ds(at * PAD_FF, PAD_FF)]))

    sums = ReduceTokens(copies, make, y, core, own, sib, got_sib, out, got)
    sums.run()
    grad_block(0, normed2, gate_act)
    grad_gain[...] = jnp.zeros_like(grad_gain)

    def back(rows, total):
        moved, terms = norm_back_rows(total, middle[rows], gains[1:2])
        grad_gain[...] += terms[:8] + terms[8:]
        value = top[rows].astype(F32) + moved
        grad_middle[rows] = value
        low[rows] = value.astype(BF16)

    sums.each(back)
    gather = GatherTokens(copies, low, middle_low, y, core)
    layers = ReduceTokens(
        copies,
        part_maker([(hidden, weights, slice(2 * PAD_FF, 3 * PAD_FF))], y, core),
        y,
        core,
        own,
        sib2,
        got_sib2,
        out2,
        got2,
    )
    for k in (2, 1, -1, 0):
        layers.part(k)
    grad_block(1, normed2, up_act)
    gather.forward()
    for k in (2, 1, -1, 0):
        layers.shared[k].wait_recv()
    layers.ring.far()
    layers.ring.direct(1)
    layers.ring.direct(-1)
    gather.near()
    gather.far()
    grad_block(2, grad_low, hidden)
    layers.ring.onward(1)
    layers.ring.onward(-1)

    def add(rows, total):
        layer[rows] = (middle[rows] + total).astype(BF16)

    layers.each(add)
    wait = copies.swap(layer, layer_out, partner, swaps)
    gather.finish()
    stored[-1].wait()
    wait()
    copies.finish()


def back_kernel(
    low_in,
    normed_in,
    att,
    qs,
    ks,
    values,
    attended,
    shares,
    raw,
    grad_middle,
    gains,
    grad_gain2,
    mlp_in,
    att_out,
    mlp_out,
    grad_in,
    gain_out,
    tokens,
    mlp,
    parts,
    grad_numer,
    grad_denom,
    grad_q,
    grad_k,
    grad_v,
    grad_qk,
    grad_values,
    own,
    sib,
    got_sib,
    out,
    got,
    mlp_out1,
    mlp_got1,
    mlp_mid,
    mlp_out2,
    mlp_got2,
    att_out1,
    att_got1,
    att_mid,
    att_out2,
    att_got2,
    mlp_sum,
    att_sum,
    last,
    gain_part,
    gain_got,
    gain_sum,
    gain_back,
    send,
    recv,
):
    x, y, z, core = place()
    zhi = z // 2
    partner = {"core": 1 - core, "zhi": 1 - zhi}
    swaps = core != zhi
    copies = Copies(send, recv)
    load_mlp = copies.local(mlp_in, mlp)
    load_low = copies.local(low_in, tokens)
    peers = group_peers(y, core)
    planes = [
        (lax.rem(x + dx, 4), lax.rem(z + dz, 4))
        for dx in range(4)
        for dz in range(4)
        if (dx, dz) != (0, 0)
    ]
    greet(
        [{"core": c, "y": d} for c, d in peers] + [at_xz(a, b) for a, b in planes], partner, swaps
    )
    load_mlp.wait()
    mlp_plane = ReducePlane(
        copies, mlp, x, z, core, mlp_out1, mlp_got1, mlp_mid, mlp_out2, mlp_got2
    )
    mlp_stages = iter(mlp_plane.stages())
    next(mlp_stages)()
    load_low.wait()

    @pl.loop(0, 4)
    def _(chip):
        rows = chip_rows(chip)
        grad_mixed = nn(tokens[rows], att[:, OUT_AT]).astype(BF16).astype(F32)
        numer = grad_mixed * shares[rows]
        grad_numer[rows] = numer.astype(BF16)
        product = numer * attended[rows].astype(F32)
        for head in range(2):
            lanes = slice(head * HEAD_V, (head + 1) * HEAD_V)
            total = -jnp.sum(product[:, lanes], axis=-1, keepdims=True)
            grad_denom[rows, lanes] = jnp.broadcast_to(total, (256, HEAD_V))

    @pl.loop(0, tokens.shape[1] // TILE)
    def _(tile):
        columns = pl.ds(pl.multiple_of(tile * TILE, TILE), TILE)
        parts[columns, OUT_AT] = tn(tokens[:, columns], attended[...]).astype(BF16)

    load_normed = copies.local(normed_in, tokens)
    grad_k[...] = jnp.zeros_like(grad_k)
    grad_v[...] = jnp.zeros_like(grad_v)
    for head in range(2):
        lanes = slice(head * HEAD_V, (head + 1) * HEAD_V)
        for block in range(4):
            rows, extent = slice(block * 256, (block + 1) * 256), (block + 1) * 256
            q = jnp.where(head_lanes(head), qs[rows], 0)
            k = ks[0:extent]
            half, scores, keep = scores_of(q, k, block, extent)
            numer = grad_numer[rows, lanes]
            grad_scores = nt(numer, values[0:extent, lanes]) + grad_denom[rows, head * HEAD_V : head * HEAD_V + 1]
            grad_s = jnp.where(keep, grad_scores * (0.25 + 0.25 * half), 0.0).astype(BF16)
            moved = nn(grad_s, k)
            if head == 0:
                grad_q[rows] = jnp.where(head_lanes(0), moved, 0.0)
            else:
                grad_q[rows] += jnp.where(head_lanes(1), moved, 0.0)
            grad_k[0:extent] += tn(grad_s, q)
            grad_v[0:extent, lanes] += tn(scores.astype(BF16), numer)
        next(mlp_stages)()
        next(mlp_stages)()

    def join(rows):
        grad_qk[rows] = (grad_q[rows] + pltpu.roll(grad_k[rows], 32, 1)).astype(BF16)
        grad_values[rows] = grad_v[rows].astype(BF16)

    row_steps(0, 1024, join, 128)
    sums = ReduceTokens(
        copies,
        part_maker([(grad_values, att, VALUE_AT), (grad_qk, att, QK_AT)], y, core),
        y,
        core,
        own,
        sib,
        got_sib,
        out,
        got,
    )
    sums.run()
    load_normed.wait()

    @pl.loop(0, tokens.shape[1] // TILE)
    def _(tile):
        columns = pl.ds(pl.multiple_of(tile * TILE, TILE), TILE)
        left = tokens[:, columns]
        parts[columns, VALUE_AT] = tn(left, grad_values[...]).astype(BF16)
        parts[columns, QK_AT] = tn(left, grad_qk[...]).astype(BF16)

    att_plane = ReducePlane(
        copies, parts, x, z, core, att_out1, att_got1, att_mid, att_out2, att_got2
    )
    att_stages = iter(att_plane.stages())
    next(att_stages)()
    for _ in range(2):
        next(mlp_stages)()
    gain_part[...] = jnp.zeros_like(gain_part)

    def back(rows, total):
        moved, terms = norm_back_rows(total, raw[rows].astype(F32), gains[0:1])
        gain_part[...] += terms[:8] + terms[8:]
        last[rows] = (grad_middle[rows] + moved).astype(BF16)

    sums.each(back)
    wait_in = copies.swap(last, grad_in, partner, swaps)
    row = lax.broadcasted_iota(jnp.int32, (8, 1), 0)
    gain_part[...] = jnp.where(
        row == 0,
        jnp.sum(gain_part[...], axis=0, keepdims=True),
        jnp.where(row == 1, jnp.sum(grad_gain2[...], axis=0, keepdims=True), 0.0),
    )
    here = 4 * z + x

    def lanes_of(block):
        return pl.ds(pl.multiple_of(block * 128, 128), 128)

    gain_copies = [
        copies.start(gain_part.at[:, lanes_of(4 * b + a)], gain_got.at[here], at_xz(a, b))
        for a, b in planes
    ]
    gain_own = copies.local(gain_part.at[:, lanes_of(here)], gain_got.at[here])
    for _ in range(4):
        next(att_stages)()
    for stage in mlp_stages:
        stage()
    for stage in att_stages:
        stage()
    me = core * 4 + y

    def take(target):
        def act(rows, total):
            target[rows] = total.astype(BF16)

        return act

    mlp_plane.each(take(mlp_sum))
    back_copies, local = [], []

    def send_back(sums_ref, out_ref):
        def cut(index):
            return sums_ref.at[pl.ds(pl.multiple_of(index * 16, 16), 16)]

        local.append(copies.local(cut(me), out_ref.at[me]))
        for c, d in peers:
            back_copies.append(copies.start(cut(c * 4 + d), out_ref.at[me], {"core": c, "y": d}))

    send_back(mlp_sum, mlp_out)
    for copy in gain_copies:
        copy.wait_recv()
    gain_own.wait()
    gain_sum[...] = jnp.sum(gain_got[...], axis=0)
    for c, d in peers:
        back_copies.append(copies.start(gain_sum, gain_back.at[me], {"core": c, "y": d}))
    local.append(copies.local(gain_sum, gain_back.at[me]))
    att_plane.each(take(att_sum))
    send_back(att_sum, att_out)
    for copy in back_copies:
        copy.wait_recv()
    for copy in local:
        copy.wait()
    gain_out[...] = jnp.sum(gain_back[...], axis=0)
    wait_in()
    copies.finish()


def unpack_kernel(
    att, mlp, layer, last, hot, query, key, value, out, gate, up, down, layer_out, grad_in
):
    here = gate.shape[1] // 8
    for block in range(8):
        for at, grad in enumerate((gate, up, down)):
            cut = mlp[block, :, at * PAD_FF : at * PAD_FF + here]
            grad[:, block * here : (block + 1) * here] = cut.astype(F32)
        value[:, block * 256 : (block + 1) * 256] = att[block, :, VALUE_AT].astype(F32)
        out[:, block * 256 : (block + 1) * 256] = att[block, :, OUT_AT].astype(F32)
        query[:, block * 32 : (block + 1) * 32] = att[block, :, 512:544].astype(F32)
        key[:, block * 32 : (block + 1) * 32] = att[block, :, 544:576].astype(F32)
    runs = layer.shape[1] // 256
    for run in range(runs):
        for source, target in ((layer, layer_out), (last, grad_in)):
            low = source[:, run * 128 : (run + 1) * 128]
            high = source[:, (runs + run) * 128 : (runs + run + 1) * 128]
            both = jnp.concatenate((low, high), axis=1)
            target[:, run * 256 : (run + 1) * 256] = nn(both, hot[...]).astype(target.dtype)


HBM, VMEM = pl.ANY, pltpu.VMEM


def call(kernel, number, ins, outs, scratch, sems, flops):
    def spec(space):
        return pl.BlockSpec(memory_space=space)

    remote = {}
    if number is not None:
        scratch = list(scratch) + [pltpu.SemaphoreType.DMA((sems,)), pltpu.SemaphoreType.DMA((sems,))]
        remote = dict(collective_id=number, has_side_effects=True)
    return pl.pallas_call(
        kernel,
        out_shape=[jax.ShapeDtypeStruct(shape, dtype) for shape, dtype, _ in outs],
        in_specs=[spec(space) for _, space in ins],
        out_specs=[spec(space) for _, _, space in outs],
        scratch_shapes=scratch,
        compiler_params=pltpu.CompilerParams(vmem_limit_bytes=VMEM_LIMIT, **remote),
        cost_estimate=pl.CostEstimate(flops=flops, bytes_accessed=2**26, transcendentals=0),
        name=kernel.__name__,
    )(*[array for array, _ in ins])


def ring_scratch(width, own=True):
    sums = [VMEM((4, 128, width), F32)] if own else []
    return sums + [
        VMEM((4, 128, width), BF16),
        VMEM((4, 128, width), BF16),
        VMEM((3, 128, width), BF16),
        VMEM((3, 128, width), BF16),
    ]


def plane_scratch(width):
    return [
        VMEM((4, 1, 128, width), BF16),
        VMEM((4, 3, 128, width), BF16),
        VMEM((4, 128, width), BF16),
        VMEM((1, 128, width), BF16),
        VMEM((3, 128, width), BF16),
    ]


def body(
    hidden_in,
    norm1_gain,
    query_weight,
    key_weight,
    value_weight,
    out_weight,
    norm2_gain,
    gate_weight,
    up_weight,
    down_weight,
    cotangent,
    source_id,
    source_counts,
):
    rows, toks, width = hidden_in.shape
    depth, ff = gate_weight.shape
    length, held = 8 * toks, 8 * depth
    mlp_w = 3 * PAD_FF
    scale = row_scale(source_id, source_counts).reshape(1, 1)
    att, mlp, raw, top = call(
        spread_kernel,
        0,
        [
            (array, VMEM)
            for array in (
                hidden_in.reshape(toks, width),
                cotangent.reshape(toks, width),
                scale,
                lane_order(False),
                query_weight,
                key_weight,
                value_weight,
                out_weight,
                gate_weight,
                up_weight,
                down_weight,
                jnp.stack((norm1_gain, norm2_gain), axis=1),
            )
        ],
        [
            ((8, depth, ATT_W), BF16, HBM),
            ((8, depth, mlp_w), BF16, HBM),
            ((toks, width), BF16, HBM),
            ((toks, width), BF16, HBM),
        ],
        [
            VMEM((8, depth, ATT_W), BF16),
            VMEM((8, depth, mlp_w), BF16),
            VMEM((toks, width), BF16),
            VMEM((toks, width), BF16),
        ],
        20,
        0,
    )
    weights = lax.all_gather(mlp.reshape(held, mlp_w), CHIPS, axis=0, tiled=True)
    att, normed, low, qs, ks, values, attended, shares, gains, middle, normed2 = call(
        forward_kernel,
        1,
        [(raw, VMEM), (att.reshape(held, ATT_W), VMEM), (top, HBM)],
        [
            ((width, ATT_W), BF16, HBM),
            ((length, width), BF16, HBM),
            ((length, width), BF16, HBM),
            ((length, 128), BF16, VMEM),
            ((length, 128), BF16, VMEM),
            ((length, 256), BF16, VMEM),
            ((length, 256), BF16, VMEM),
            ((length, 256), F32, VMEM),
            ((8, width), F32, VMEM),
            ((toks, width), F32, VMEM),
            ((length, width), BF16, HBM),
        ],
        [
            VMEM((length, width), BF16),
            VMEM((width, ATT_W), BF16),
            VMEM((length, width), BF16),
        ]
        + ring_scratch(width)
        + [VMEM((toks, width), BF16)],
        140,
        4 * 10**9,
    )
    grad_middle, grad_gain2, middle_low, grads, layer = call(
        mlp_kernel,
        2,
        [
            (normed2, HBM),
            (low, HBM),
            (weights, HBM),
            (middle, VMEM),
            (top, VMEM),
            (gains, VMEM),
        ],
        [
            ((toks, width), F32, VMEM),
            ((8, width), F32, VMEM),
            ((length, width), BF16, HBM),
            ((width, mlp_w), BF16, HBM),
            ((toks, width), BF16, HBM),
        ],
        [
            VMEM((length, width), BF16),
            VMEM((length, width), BF16),
            VMEM((width, mlp_w), BF16),
            VMEM((length, PAD_FF), BF16),
            VMEM((length, PAD_FF), BF16),
            VMEM((length, PAD_FF), BF16),
            VMEM((width, PAD_FF), BF16),
        ]
        + ring_scratch(width)
        + ring_scratch(width, own=False)
        + [VMEM((toks, width), BF16), VMEM((toks, width), BF16)],
        80,
        30 * 10**9,
    )
    att_back, mlp_back, last, gain_sums = call(
        back_kernel,
        3,
        [
            (middle_low, HBM),
            (normed, HBM),
            (att, VMEM),
            (qs, VMEM),
            (ks, VMEM),
            (values, VMEM),
            (attended, VMEM),
            (shares, VMEM),
            (raw, VMEM),
            (grad_middle, VMEM),
            (gains, VMEM),
            (grad_gain2, VMEM),
            (grads, HBM),
        ],
        [
            ((8, depth, ATT_W), BF16, HBM),
            ((8, depth, mlp_w), BF16, HBM),
            ((toks, width), BF16, HBM),
            ((8, 128), F32, VMEM),
        ],
        [
            VMEM((length, width), BF16),
            VMEM((width, mlp_w), BF16),
            VMEM((width, ATT_W), BF16),
            VMEM((length, 256), BF16),
            VMEM((length, 256), F32),
            VMEM((length, 128), F32),
            VMEM((length, 128), F32),
            VMEM((length, 256), F32),
            VMEM((length, 128), BF16),
            VMEM((length, 256), BF16),
        ]
        + ring_scratch(width)
        + plane_scratch(mlp_w)
        + plane_scratch(ATT_W)
        + [
            VMEM((held, mlp_w), BF16),
            VMEM((held, ATT_W), BF16),
            VMEM((toks, width), BF16),
            VMEM((8, width), F32),
            VMEM((16, 8, 128), F32),
            VMEM((8, 128), F32),
            VMEM((8, 8, 128), F32),
        ],
        200,
        8 * 10**9,
    )
    grads_out = call(
        unpack_kernel,
        None,
        [(array, VMEM) for array in (att_back, mlp_back, layer, last, lane_order(True))],
        [
            ((depth, query_weight.shape[1]), F32, VMEM),
            ((depth, key_weight.shape[1]), F32, VMEM),
            ((depth, value_weight.shape[1]), F32, VMEM),
            ((depth, out_weight.shape[1]), F32, VMEM),
            ((depth, ff), F32, VMEM),
            ((depth, ff), F32, VMEM),
            ((depth, ff), F32, VMEM),
            ((toks, width), BF16, VMEM),
            ((toks, width), F32, VMEM),
        ],
        [],
        0,
        0,
    )
    grad_query, grad_key, grad_value, grad_out, grad_gate, grad_up, grad_down = grads_out[:7]
    at = (lax.axis_index("core") * 4 + lax.axis_index("y")) * depth
    pair = lax.dynamic_slice(gain_sums, (0, at), (8, depth))
    return (
        grads_out[7].reshape(rows, toks, width),
        grads_out[8].reshape(rows, toks, width),
        pair[0],
        grad_query,
        grad_key,
        grad_value,
        grad_out,
        pair[1],
        grad_gate,
        grad_up,
        grad_down,
    )


def solution(mesh):
    zlo, chips_x, cores, chips_y, zhi = 2, 4, 2, 4, 2
    whole = Mesh(mesh.devices.reshape(zlo, chips_x, cores, chips_y, zhi), AXES)
    weight = P(AXES, None)
    gain = P(AXES)
    tokens = P(DP, SEQ, None)
    return jax.shard_map(
        body,
        mesh=whole,
        in_specs=(
            tokens,
            gain,
            weight,
            weight,
            weight,
            weight,
            gain,
            weight,
            weight,
            weight,
            tokens,
            P(DP),
            P(),
        ),
        out_specs=(
            tokens,
            tokens,
            gain,
            weight,
            weight,
            weight,
            weight,
            gain,
            weight,
            weight,
            weight,
        ),
        check_vma=False,
    )
```

time: 721 us -> 333 us (0.46)
  waiting for transfers between devices: 472 us -> 0.04 us
  Pallas kernels: 0 us -> 313 us
  matrix products: 105 us -> 0 us
  local copies, waits for them, and re-layouts: 44.5 us -> 1.96 us
  starting transfers between devices: 32.4 us -> 0.04 us
  other arithmetic: 28.3 us -> 1.98 us
  blocking collectives: 17.6 us -> 0 us
    pallas_call x0 -> x5, Pallas kernels: none -> 313 us  [call(): pl.pallas_call(kernel, out_shape=[jax.ShapeDtypeStruct(shape, dtype) for...]
    reduce_scatter x6 -> x0, waiting for transfers between devices: 242 us -> none  [the longest x4 83.7 us: own_rows(): lax.psum_scatter(total.astype(jnp.bfloat16), TOKENS, scatter_dimension=0,...]
    all_gather x6 -> x1, waiting for transfers between devices: 200 us -> 0.02 us  [body(): lax.all_gather(mlp.reshape(held, mlp_w), CHIPS, axis=0, tiled=True)]
    dot_general x31 -> x0, matrix products: 105 us -> none  [the longest x11 37.8 us: dot(): return jnp.dot(left, right, preferred_element_type=jnp.float32)]
    unnamed x115 -> x0, local copies, waits for them, and re-layouts: 26.6 us -> none
    ppermute x4 -> x0, starting transfers between devices: 24.2 us -> none  [swap(): lax.ppermute(array, ('core', 'zhi'), [(0, 0), (1, 2), (2, 1), (3, 3)])]
    ppermute x4 -> x0, waiting for transfers between devices: 21 us -> none  [swap(): lax.ppermute(array, ('core', 'zhi'), [(0, 0), (1, 2), (2, 1), (3, 3)])]
    all_to_all x1 -> x0, blocking collectives: 17.6 us -> none  [body(): lax.all_to_all(pack, COLUMNS, split_axis=0, concat_axis=0, tiled=True)]
  transfers between devices with their start and end apart: 17 -> 1, of which waited for: 14 -> 0; matrix products, arithmetic and copies ran while one was open for 12% -> 0% of each run, Pallas kernels for 0% -> 29%
where the time goes in v3:
time: 333 us; the launch traced here: 332 us
  Pallas kernels  313 us (94%)
  between operations  15.4 us (5%)
    pallas_call x5, Pallas kernels, call(): pl.pallas_call(kernel, out_shape=[jax.ShapeDtypeStruct(shape, dtype) for...  313 us
  transfers between devices with their start and end apart: 1, of which 0 were waited for; matrix products, arithmetic and copies ran while one was open for 0% of the time, Pallas kernels for 29%

profile of v3, /device:TPU:1, one launch (start us, length us, event | category | flops | bytes accessed | tf_op | source)
XLA Modules:
  0.0 332.3 jit_solution(9074056206861047812)
XLA Ops:
  7.2 0.0 all-gather.2.cloned.1.call-start
  7.2 0.7 pad_maximum_fusion
  7.9 0.7 copy.28.gains
  9.2 1.3 fusion
  11.2 23.2 %spread_kernel.1 = (bf16[8,16,640]{2,1,0:T(8,128)(2,1)}, bf16[8,16,2304]{2,1,0:T(8,128)(2,1)}, bf16[128,2048]{1,0:T(8,128)(2,1)}, bf16[128,2048]{1,0:T(8,128)(2,1)}) custom-call(bf16[128,2048]{1,0:T(8,128)(2,1)} %bitcast.16, bf16[128,2048]{1,0:T(8,128)(2,1)} %bitcast.17, f32[1,1]{1,0:T(1,128)} %bitcast.3.scale, bf16[256,256]{1,0:T(8,128)(2,1)} %constant.24.clone.hot, ...), custom_call_target="tpu_custom_call" | custom-call | bytes 67108864 | tf_op jit(solution)/shard_map/spread_kernel/pallas_call | solution.py:1143
  34.5 0.0 all-gather.2.cloned.1.call-update
  34.5 96.2 %forward_kernel.1 = (bf16[2048,640]{1,0:T(8,128)(2,1)}, bf16[1024,2048]{1,0:T(8,128)(2,1)}, bf16[1024,2048]{1,0:T(8,128)(2,1)}, bf16[1024,128]{1,0:T(8,128)(2,1)...) custom-call(bf16[128,2048]{1,0:T(8,128)(2,1)} %get-tuple-element.44., ...), custom_call_target="tpu_custom_call" | custom-call | flops 4000000000 | bytes 67108864 | tf_op jit(solution)/shard_map/forward_kernel/pallas_call | solution.py:1143
  130.7 0.0 all-gather.2.cloned.1.call-done.weights_in
  130.7 98.1 %mlp_kernel.1 = (f32[128,2048]{1,0:T(8,128)}, f32[8,2048]{1,0:T(8,128)}, bf16[1024,2048]{1,0:T(8,128)(2,1)}, bf16[2048,2304]{1,0:T(8,128)(2,1)}, bf16[128,2048]{1,0:T(8,128)(2,1)}) custom-call(bf16[1024,2048]{1,0:T(8,128)(2,1)} %get-tuple-element.47.normed2_in, bf16[1024,2048]{1,0:T(8,128)(2,1)} %get-tuple-element.48.low_in, ...), custom_call_target="tpu_custom_call" | custom-call | flops 30000001024 | bytes 67108864 | tf_op jit(solution)/shard_map/mlp_kernel/pallas_call | solution.py:1143
  228.8 91.9 %back_kernel.1 = (bf16[8,16,640]{2,1,0:T(8,128)(2,1)}, bf16[8,16,2304]{2,1,0:T(8,128)(2,1)}, bf16[128,2048]{1,0:T(8,128)(2,1)}, f32[8,128]{1,0:T(8,128)}) custom-call(bf16[1024,2048]{1,0:T(8,128)(2,1)} %get-tuple-element.52.low_in, bf16[1024,2048]{1,0:T(8,128)(2,1)} %get-tuple-element.53.normed_in, bf16[2048,640]{1,0:T(8,128)(2,1)} %get-tuple-element.54.att, ...), custom_call_target="tpu_custom_call" | custom-call | flops 8000000000 | bytes 67108864 | tf_op jit(solution)/shard_map/back_kernel/pallas_call | solution.py:1143
  320.7 0.8 constant_dynamic-slice_fusion
  321.5 0.5 slice_bitcast_fusion
  322.0 3.5 %unpack_kernel.1 = (f32[16,256]{1,0:T(8,128)}, f32[16,256]{1,0:T(8,128)}, f32[16,2048]{1,0:T(8,128)}, f32[16,2048]{1,0:T(8,128)}, f32[16,5504]{1,0:T(8,128)}, /*...) custom-call(bf16[8,16,640]{2,1,0:T(8,128)(2,1)} %get-tuple-element.63.att, ...), custom_call_target="tpu_custom_call" | custom-call | bytes 67108864 | tf_op jit(solution)/shard_map/unpack_kernel/pallas_call | solution.py:1143
Async XLA Ops:
  7.2 123.5 %all-gather.2.cloned.1.call-start = ((), (), s32[]{:S(2)}) async-start(), calls=%async_computation | async-start | bytes 10027008 | tf_op jit(solution)/shard_map/all_gather | solution.py:1230
Sparse Core Ops, SparseCore 0:
  34.6 76.0 all-gather.1
